TPU v7x, 32 devices: a whole 2x2x4 slice. The times are simulated.
32 devices in a mesh: wide: 16 (over z, x, core), narrow: 2 (over y).
Axes of the slice: x: 2, y: 2, z: 4, core: 2. Of those that a mesh axis runs over, the one named last changes fastest.
Arguments:
- patches: bfloat16 [128, 324, 512], P(('wide', 'narrow')), may hold values from -6 to 6
- cotangent: bfloat16 [128, 324, 512], P(('wide', 'narrow')), may hold values from -6 to 6
- size_class: int32 [128], P(('wide', 'narrow')), may hold values from 0 to 2
- w_in: bfloat16 [2, 1572864], P(None, ('wide', 'narrow')), may hold values from -0.25 to 0.25
- w_out: bfloat16 [2, 786432], P(None, ('wide', 'narrow')), may hold values from -0.15625 to 0.15625
- spatial: bfloat16 [2, 105312], P(None, ('wide', 'narrow')), as said below
- vectors: bfloat16 [2, 7680], P(None, ('wide', 'narrow')), as said below
Outputs:
- outputs: float32 [128, 324, 512], P(('wide', 'narrow'))
- patch_grad: float32 [128, 324, 512], P(('wide', 'narrow'))
- grad_w_in: float32 [2, 1572864], P(None, ('wide', 'narrow'))
- grad_w_out: float32 [2, 786432], P(None, ('wide', 'narrow'))
- grad_spatial: float32 [2, 105312], P(None, ('wide', 'narrow'))
- grad_vectors: float32 [2, 7680], P(None, ('wide', 'narrow'))
Inputs may be any that keep to these rules, and one draw needn't show every extreme that they name: `spatial`: entries past the 324 x 324 matrix and 324 bias are never read. Entries past the six vectors are never read.
All inputs are finite; a program needn't handle non-finite values.
Results may differ from a plain program's by a relative error of at most 0.009.
Values may be sent and summed in bfloat16 or wider, within the bound.
No kernel may reach another device: no remote copies, remote signals or barrier semaphores. Data moves between devices by JAX's collectives and lax.ppermute only.
A program may use at most 192 MiB of HBM per device.

v0:
```python
import jax
import jax.numpy as jnp
from jax import lax
from jax.sharding import PartitionSpec as P

D = 512
H = 3072
P_SIZE = 324
LAYERS = 2
G = 1536


EPS = 1e-05


def norm_rows(value, gain, shift):
    mean = jnp.mean(value, axis=-1, keepdims=True)
    centred = value - mean
    spread = jnp.mean(centred * centred, axis=-1, keepdims=True)
    factor = lax.rsqrt(spread + EPS)
    normed = centred * factor
    return (normed * gain + shift, normed, factor)


def norm_back(grad, normed, factor, gain):
    scaled = grad * gain
    inner = scaled - jnp.mean(scaled, axis=-1, keepdims=True)
    inner = inner - normed * jnp.mean(scaled * normed, axis=-1, keepdims=True)
    return factor * inner


def gelu_tanh(value):
    return jax.nn.gelu(value, approximate=True)


def unpack(pieces):
    w_in_full, w_out_full, sp_full, vec_full = pieces
    vec = vec_full.astype(jnp.float32)
    parts = {
        "w_in": w_in_full.reshape(D, H),
        "w_out": w_out_full.reshape(G, D),
        "sp_mat": sp_full[0 : P_SIZE * P_SIZE].reshape(P_SIZE, P_SIZE),
        "sp_bias": sp_full[P_SIZE * P_SIZE : P_SIZE * P_SIZE + P_SIZE].astype(jnp.float32),
        "ln1_gain": vec[0:D],
        "ln1_shift": vec[D : 2 * D],
        "in_bias": vec[2 * D : 2 * D + H],
        "ln2_gain": vec[2 * D + H : 2 * D + H + G],
        "ln2_shift": vec[2 * D + H + G : 2 * D + H + 2 * G],
        "out_bias": vec[2 * D + H + 2 * G : 3 * D + H + 2 * G],
    }
    return parts


def forward_layer(resid, mask, parts):
    ln1_out, ln1_hat, ln1_factor = norm_rows(resid, parts["ln1_gain"], parts["ln1_shift"])
    normed_low = ln1_out.astype(jnp.bfloat16)
    pre = (
        jnp.einsum("bpd,dh->bph", normed_low, parts["w_in"], preferred_element_type=jnp.float32)
        + parts["in_bias"]
    )
    act = gelu_tanh(pre)
    upper = act[..., :G]
    ln2_out, ln2_hat, ln2_factor = norm_rows(act[..., G:], parts["ln2_gain"], parts["ln2_shift"])
    mixed_in = (ln2_out * mask).astype(jnp.bfloat16)
    mixed = jnp.einsum("ij,bjc->bic", parts["sp_mat"], mixed_in, preferred_element_type=jnp.float32)
    gate = mask * (mixed + parts["sp_bias"][None, :, None])
    gated = (upper * gate).astype(jnp.bfloat16)
    branch = (
        jnp.einsum("bpc,cd->bpd", gated, parts["w_out"], preferred_element_type=jnp.float32)
        + parts["out_bias"]
    )
    kept = (ln1_hat, ln1_factor, normed_low, pre, upper, gate, ln2_hat, ln2_factor, mixed_in, gated)
    return (mask * (resid + branch), kept)


def backward_layer(grad_next, mask, parts, kept, vec_len, sp_len):
    ln1_hat, ln1_factor, normed_low, pre, upper, gate, ln2_hat, ln2_factor, mixed_in, gated = kept
    masked = grad_next * mask
    grad_branch = masked.astype(jnp.bfloat16)
    g_out_bias = jnp.sum(grad_branch.astype(jnp.float32), axis=(0, 1))
    g_w_out = jnp.einsum("bpc,bpd->cd", gated, grad_branch, preferred_element_type=jnp.float32)
    grad_gated = jnp.einsum(
        "bpd,cd->bpc", grad_branch, parts["w_out"], preferred_element_type=jnp.float32
    )
    grad_upper = grad_gated * gate
    grad_mix = (grad_gated * upper).astype(jnp.bfloat16) * mask.astype(jnp.bfloat16)
    g_sp_bias = jnp.sum(grad_mix.astype(jnp.float32), axis=(0, 2))
    g_sp_mat = jnp.einsum("bic,bjc->ij", grad_mix, mixed_in, preferred_element_type=jnp.float32)
    grad_ln2 = (
        jnp.einsum("ij,bic->bjc", parts["sp_mat"], grad_mix, preferred_element_type=jnp.float32)
        * mask
    )
    g_ln2_gain = jnp.sum(grad_ln2 * ln2_hat, axis=(0, 1))
    g_ln2_shift = jnp.sum(grad_ln2, axis=(0, 1))
    grad_lower = norm_back(grad_ln2, ln2_hat, ln2_factor, parts["ln2_gain"])
    grad_act = jnp.concatenate([grad_upper, grad_lower], axis=-1)
    unused, pull = jax.vjp(gelu_tanh, pre)
    grad_pre = pull(grad_act)[0].astype(jnp.bfloat16)
    g_in_bias = jnp.sum(grad_pre.astype(jnp.float32), axis=(0, 1))
    g_w_in = jnp.einsum("bpd,bph->dh", normed_low, grad_pre, preferred_element_type=jnp.float32)
    grad_ln1 = jnp.einsum(
        "bph,dh->bpd", grad_pre, parts["w_in"], preferred_element_type=jnp.float32
    )
    g_ln1_gain = jnp.sum(grad_ln1 * ln1_hat, axis=(0, 1))
    g_ln1_shift = jnp.sum(grad_ln1, axis=(0, 1))
    grad_resid = masked + norm_back(grad_ln1, ln1_hat, ln1_factor, parts["ln1_gain"])
    vec_used = 3 * D + H + 2 * G
    g_vec = jnp.concatenate(
        [
            g_ln1_gain,
            g_ln1_shift,
            g_in_bias,
            g_ln2_gain,
            g_ln2_shift,
            g_out_bias,
            jnp.zeros((vec_len - vec_used,), jnp.float32),
        ]
    )
    g_sp = jnp.concatenate(
        [
            g_sp_mat.reshape(-1),
            g_sp_bias,
            jnp.zeros((sp_len - P_SIZE * P_SIZE - P_SIZE,), jnp.float32),
        ]
    )
    return (grad_resid, (g_w_in.reshape(-1), g_w_out.reshape(-1), g_sp, g_vec))


def per_device(patches, cotangent, size_class, w_in, w_out, spatial, vectors):
    count_all = lax.axis_size(("wide", "narrow"))
    sp_len = spatial.shape[1] * count_all
    vec_len = vectors.shape[1] * count_all
    counts = (
        100 + 96 * (size_class >= 1).astype(jnp.int32) + 128 * (size_class >= 2).astype(jnp.int32)
    )
    places = lax.broadcasted_iota(jnp.int32, (patches.shape[0], P_SIZE, 1), 1)
    mask = (places < counts[:, None, None]).astype(jnp.float32)
    resid = patches.astype(jnp.float32)
    gathered = []
    stored = []
    for layer in range(LAYERS):
        pieces = (
            lax.all_gather(w_in[layer], ("wide", "narrow"), axis=0, tiled=True),
            lax.all_gather(w_out[layer], ("wide", "narrow"), axis=0, tiled=True),
            lax.all_gather(spatial[layer], ("wide", "narrow"), axis=0, tiled=True),
            lax.all_gather(vectors[layer], ("wide", "narrow"), axis=0, tiled=True),
        )
        gathered.append(pieces)
        resid, kept = forward_layer(resid, mask, unpack(pieces))
        stored.append(kept)
    grad = cotangent.astype(jnp.float32)
    shard_grads = [None] * LAYERS
    for layer in reversed(range(LAYERS)):
        pieces = (
            lax.all_gather(w_in[layer], ("wide", "narrow"), axis=0, tiled=True),
            lax.all_gather(w_out[layer], ("wide", "narrow"), axis=0, tiled=True),
            lax.all_gather(spatial[layer], ("wide", "narrow"), axis=0, tiled=True),
            lax.all_gather(vectors[layer], ("wide", "narrow"), axis=0, tiled=True),
        )
        grad, layer_grads = backward_layer(
            grad, mask, unpack(pieces), stored[layer], vec_len, sp_len
        )
        shard_grads[layer] = (
            lax.psum_scatter(layer_grads[0], ("wide", "narrow"), scatter_dimension=0, tiled=True),
            lax.psum_scatter(layer_grads[1], ("wide", "narrow"), scatter_dimension=0, tiled=True),
            lax.psum_scatter(layer_grads[2], ("wide", "narrow"), scatter_dimension=0, tiled=True),
            lax.psum_scatter(layer_grads[3], ("wide", "narrow"), scatter_dimension=0, tiled=True),
        )
    result = tuple(
        (jnp.stack([shard_grads[layer][index] for layer in range(LAYERS)]) for index in range(4))
    )
    return (resid, grad, result[0], result[1], result[2], result[3])


def solution(mesh):
    return jax.shard_map(
        per_device,
        mesh=mesh,
        in_specs=(
            P(("wide", "narrow"), None, None),
            P(("wide", "narrow"), None, None),
            P(("wide", "narrow")),
            P(None, ("wide", "narrow")),
            P(None, ("wide", "narrow")),
            P(None, ("wide", "narrow")),
            P(None, ("wide", "narrow")),
        ),
        out_specs=(
            P(("wide", "narrow"), None, None),
            P(("wide", "narrow"), None, None),
            P(None, ("wide", "narrow")),
            P(None, ("wide", "narrow")),
            P(None, ("wide", "narrow")),
            P(None, ("wide", "narrow")),
        ),
        check_vma=False,
    )
```

profile of v0, /device:TPU:0, one launch (start us, length us, event | category | flops | bytes accessed | tf_op | source)
XLA Modules:
  0.0 1019.0 jit_solution(13129482002994577509)
XLA Ops:
  16.2 42.3 %all-reduce.14 = (bf16[7680]{0:T(1024)(128)(2,1)S(1)}, bf16[7680]{0:T(1024)(128)(2,1)S(1)}) all-reduce(bf16[7680]{0:T(1024)(128)(2,1)S(1)} %dynamic-update-slice, bf16[7680]{0:T(1024)(128)(2,1)S(1)} %dynamic-update-slice.2), channel_id=2, replica_groups=mesh['wide'=16,'narrow'=2] {'wide','narrow'}, use_global_device_ids=true, to_apply=%add | all-reduce | flops 15360 | bytes 61440
  64.2 78.8 %all-reduce.21.cloned.1.call-done = (bf16[105312]{0:T(1024)(128)(2,1)}, bf16[105312]{0:T(1024)(128)(2,1)}) async-done(((bf16[105312]{0:T(1024)(128)(2,1)}, bf16[105312]{0:T(1024)(128)(2,1)}), (bf16[105312]{0:T(1024)(128)(2,1)}, bf16[105312]{0:T(1024)(128)(2,1)})) %all-reduce.21.cloned.1.call-update) | async-done | bytes 421264
  153.2 53.8 %all-gather.19.cloned.1.call-done = bf16[1,786432]{1,0:T(2,128)(2,1)} async-done(((bf16[1,24576]{1,0:T(2,128)(2,1)}), bf16[1,786432]{1,0:T(2,128)(2,1)}) %all-gather.19.cloned.1.call-update) | async-done | bytes 1572880 | tf_op jit(solution)/shard_map/all_gather | solution.py:144
  207.0 33.9 %reduce.17 = bf16[786432]{0:T(1024)(128)(2,1)S(1)} reduce(bf16[1,786432]{1,0:T(2,128)(2,1)} %all-gather.19.cloned.1.call-done, bf16[]{:T(256)} %constant.96), dimensions={0}, to_apply=%all-gather.7.reduce_sub_computation | reduce | bytes 3145730 | tf_op jit(solution)/shard_map/all_gather | solution.py:144
  243.2 25.1 %all-gather.15.cloned.1.call-done = bf16[1,786432]{1,0:T(2,128)(2,1)} async-done(((bf16[1,24576]{1,0:T(2,128)(2,1)}), bf16[1,786432]{1,0:T(2,128)(2,1)}) %all-gather.15.cloned.1.call-update) | async-done | bytes 1572880 | tf_op jit(solution)/shard_map/all_gather | solution.py:144
  268.2 33.7 %reduce.9 = bf16[786432]{0:T(1024)(128)(2,1)S(1)} reduce(bf16[1,786432]{1,0:T(2,128)(2,1)} %all-gather.15.cloned.1.call-done, bf16[]{:T(256)} %constant.96), dimensions={0}, to_apply=%all-gather.3.reduce_sub_computation | reduce | bytes 3145730 | tf_op jit(solution)/shard_map/all_gather | solution.py:144
  304.1 36.2 %all-gather.17.cloned.1.call-done = bf16[1,1572864]{1,0:T(2,128)(2,1)} async-done(((bf16[1,49152]{1,0:T(2,128)(2,1)}), bf16[1,1572864]{1,0:T(2,128)(2,1)}) %all-gather.17.cloned.1.call-update) | async-done | bytes 3145744 | tf_op jit(solution)/shard_map/all_gather | solution.py:143
  340.3 66.8 %reduce.11 = bf16[1572864]{0:T(1024)(128)(2,1)S(1)} reduce(bf16[1,1572864]{1,0:T(2,128)(2,1)} %all-gather.17.cloned.1.call-done, bf16[]{:T(256)} %constant.96), dimensions={0}, to_apply=%all-gather.5.reduce_sub_computation | reduce | bytes 6291458 | tf_op jit(solution)/shard_map/all_gather | solution.py:143
  411.5 66.3 %reduce.3 = bf16[1572864]{0:T(1024)(128)(2,1)S(1)} reduce(bf16[1,1572864]{1,0:T(2,128)(2,1)} %all-gather.13.cloned.1.call-done, bf16[]{:T(256)} %constant.96), dimensions={0}, to_apply=%all-gather.1.reduce_sub_computation | reduce | bytes 6291458 | tf_op jit(solution)/shard_map/all_gather | solution.py:143
  480.7 14.0 %multiply_multiply_fusion.5 = (f32[4,324,3072]{2,1,0:T(8,128)S(1)}, f32[4,324,3072]{2,1,0:T(8,128)}) fusion(f32[3072]{0:T(1024)S(1)} %bitcast.114, bf16[512,3072,1]{1,0,2:T(8,128)(2,1)} %reshape.244, f32[512]{0:T(512)S(1)} %bitcast.129, f32[512]{0:T(512)S(1)} %bitcast.118, f32[4,324]{1,0:T(4,128)S(1)} %add_rsqrt_fusion.3, ...), kind=kOutput, calls=%fused_computation.23 | convolution fusion | flops 4116676608 | bytes 36350080 | tf_op jit(solution)/shard_map/bpd,dh->bph/dot_general | solution.py:58
  510.5 13.6 %multiply_multiply_fusion.4 = (f32[4,324,3072]{2,1,0:T(8,128)S(1)}, f32[4,324,3072]{2,1,0:T(8,128)}) fusion(f32[3072]{0:T(1024)S(1)} %bitcast.116, bf16[512,3072,1]{1,0,2:T(8,128)(2,1)} %reshape.247, f32[4,324,512]{2,1,0:T(8,128)} %copy-done.6, f32[512]{0:T(512)S(1)} %bitcast.131, f32[512]{0:T(512)S(1)} %bitcast.122, f32[4,324]{1,0:T(4,128)S(1)} %add_rsqrt_fusion.1, ...), kind=kOutput, calls=%fused_computation.22 | convolution fusion | flops 4116013056 | bytes 37677184 | tf_op jit(solution)/shard_map/bpd,dh->bph/dot_general | solution.py:58
  528.1 6.5 convert_reduce_fusion.2
  540.4 6.1 fusion.15
  546.6 17.9 %subtract_multiply_fusion.1 = (f32[4,324,1536]{2,1,0:T(8,128)S(1)}, bf16[4,324,1536]{2,1,0:T(8,128)(2,1)}, f32[4,324,1536]{2,1,0:T(8,128)S(1)}) fusion(f32[4,1536,324]{1,2,0:T(8,128)} %get-tuple-element.91, f32[4,324]{1,0:T(4,128)S(1)} %get-tuple-element.95, f32[4,324]{1,0:T(4,128)S(1)} %get-tuple-element.96, f32[1536]{0:T(1024)S(1)} %get-tuple-element.32, ...), kind=kOutput, calls=%fused_computation.41 | convolution fusion | flops 1327767552 | bytes 60538880 | tf_op jit(solution)/shard_map/ij,bjc->bic/dot_general | solution.py:65
  564.5 15.9 %convert_reduce_fusion = (f32[3072]{0:T(1024)S(1)}, bf16[4,324,3072]{2,1,0:T(8,128)(2,1)}) fusion(f32[4,324,3072]{2,1,0:T(8,128)} %get-tuple-element.89, f32[3072]{0:T(1024)S(1)} %bitcast.117, f32[4,324,1536]{2,1,0:T(8,128)S(1)} %get-tuple-element.64, f32[4,324,1536]{2,1,0:T(8,128)S(1)} %get-tuple-element.67), kind=kLoop, calls=%fused_computation.20 | loop fusion | flops 95548416 | bytes 39837696 | tf_op jit(solution)/shard_map/reduce_sum | solution.py:99
  580.4 10.1 multiply_reduce_fusion.6
  590.6 7.6 convolution_bitcast_fusion
  617.4 8.8 convert_reduce_fusion.3
  634.1 8.0 fusion.14
  642.1 7.8 subtract_multiply_fusion
  650.0 14.9 %convert_reduce_fusion.1 = (f32[3072]{0:T(1024)S(1)}, bf16[4,324,3072]{2,1,0:T(8,128)(2,1)S(1)}) fusion(f32[4,324,3072]{2,1,0:T(8,128)} %get-tuple-element.83, f32[3072]{0:T(1024)S(1)} %bitcast.115, f32[4,324,1536]{2,1,0:T(8,128)S(1)} %subtract_multiply_fusion, f32[4,324,1536]{2,1,0:T(8,128)} %get-tuple-element.68), kind=kLoop, calls=%fused_computation.21 | loop fusion | flops 95548416 | bytes 39837696 | tf_op jit(solution)/shard_map/reduce_sum | solution.py:99
  701.0 6.9 fusion.36
  708.0 41.5 %all-reduce.12 = (f32[7680]{0:T(1024)S(1)}, f32[7680]{0:T(1024)S(1)}) all-reduce(f32[7680]{0:T(1024)S(1)} %constant_dynamic-update-slice_fusion.1, f32[7680]{0:T(1024)S(1)} %constant_dynamic-update-slice_fusion), channel_id=17, replica_groups=mesh['wide'=16,'narrow'=2] {'wide','narrow'}, use_global_device_ids=true, to_apply=%region_37.0.clone | all-reduce | flops 15360 | bytes 122880
  756.1 247.9 %all-reduce.19.cloned.1.call-done = (f32[1572864]{0:T(1024)}, f32[1572864]{0:T(1024)}, f32[786432]{0:T(1024)}, f32[786432]{0:T(1024)}, f32[105312]{0:T(1024)}, /*index=5*/f32[105312]{0:T(1024)}) async-done(((f32[1572864]{0:T(1024)}, f32[1572864]{0:T(1024)}, f32[786432]{0:T(1024)}, f32[786432]{0:T(1024)}, f32[105312]{0:T(1024)}, /*index=5*/f32[105312]{0:T(1024)}), (f32[1572864]{0:T(1024)}, ...) | async-done | bytes 19716880
  (228 shorter events, 139.5 us)
Async XLA Ops:
  7.2 135.8 %all-reduce.21.cloned.1.call-start = ((), (), s32[]{:S(2)}) async-start(), calls=%async_computation.5 | async-start | bytes 843776
  9.5 197.5 %all-gather.19.cloned.1.call-start = ((), (), s32[]{:S(2)}) async-start(), calls=%async_computation.3 | async-start | bytes 3244032 | tf_op jit(solution)/shard_map/all_gather | solution.py:144
  11.4 256.8 %all-gather.15.cloned.1.call-start = ((), (), s32[]{:S(2)}) async-start(), calls=%async_computation.1 | async-start | bytes 3244032 | tf_op jit(solution)/shard_map/all_gather | solution.py:144
  12.1 328.2 %all-gather.17.cloned.1.call-start = ((), (), s32[]{:S(2)}) async-start(), calls=%async_computation.2 | async-start | bytes 6488064 | tf_op jit(solution)/shard_map/all_gather | solution.py:143
  14.3 397.2 %all-gather.13.cloned.1.call-start = ((), (), s32[]{:S(2)}) async-start(), calls=%async_computation | async-start | bytes 6488064 | tf_op jit(solution)/shard_map/all_gather | solution.py:143
  14.9 989.1 %all-reduce.19.cloned.1.call-start = ((), (), s32[]{:S(2)}) async-start(), calls=%async_computation.4 | async-start | bytes 39436288
  58.6 422.1 %copy-start.26 = (f32[1,3072]{1,0:T(1,128)}, f32[1,3072]{1,0:T(1,128)S(1)}, u32[]{:S(2)}) copy-start(f32[1,3072]{1,0:T(1,128)S(1)} %slice.144) | copy-start | bytes 36868
  61.7 419.0 %copy-start.30 = (f32[1,512]{1,0:T(1,128)}, f32[1,512]{1,0:T(1,128)S(1)}, u32[]{:S(2)}) copy-start(f32[1,512]{1,0:T(1,128)S(1)} %get-tuple-element.79) | copy-start | bytes 6148
  61.7 419.0 %copy-start.34 = (f32[1,512]{1,0:T(1,128)}, f32[1,512]{1,0:T(1,128)S(1)}, u32[]{:S(2)}) copy-start(f32[1,512]{1,0:T(1,128)S(1)} %get-tuple-element.78) | copy-start | bytes 6148
  62.2 448.3 %copy-start.36 = (f32[1,512]{1,0:T(1,128)}, f32[1,512]{1,0:T(1,128)S(1)}, u32[]{:S(2)}) copy-start(f32[1,512]{1,0:T(1,128)S(1)} %get-tuple-element.75) | copy-start | bytes 6148
  62.3 418.4 %copy-start.24 = (f32[4,324]{1,0:T(4,128)}, f32[4,324]{1,0:T(4,128)S(1)}, u32[]{:S(2)}) copy-start(f32[4,324]{1,0:T(4,128)S(1)} %broadcast_multiply_fusion.11) | copy-start | bytes 15556
  64.2 416.5 %copy-start.28 = (f32[4,324]{1,0:T(4,128)}, f32[4,324]{1,0:T(4,128)S(1)}, u32[]{:S(2)}) copy-start(f32[4,324]{1,0:T(4,128)S(1)} %add_rsqrt_fusion.3) | copy-start | bytes 15556
  524.1 16.3 %copy-start.2 = (f32[4,324,3072]{2,1,0:T(8,128)}, f32[4,324,3072]{2,1,0:T(8,128)S(1)}, u32[]{:S(2)}) copy-start(f32[4,324,3072]{2,1,0:T(8,128)S(1)} %get-tuple-element.88) | copy-start | bytes 47775748
  564.5 15.9 %copy-start.7 = (f32[4,324,512]{2,1,0:T(8,128)S(1)}, f32[4,324,512]{2,1,0:T(8,128)}, u32[]{:S(2)}) copy-start(f32[4,324,512]{2,1,0:T(8,128)} %copy-done.6) | copy-start | bytes 7962628
  564.5 15.9 %copy-start.13 = (bf16[512,3072,1]{1,0,2:T(8,128)(2,1)S(1)}, bf16[512,3072,1]{1,0,2:T(8,128)(2,1)}, u32[]{:S(2)}) copy-start(bf16[512,3072,1]{1,0,2:T(8,128)(2,1)} %reshape.247) | copy-start | bytes 9437188
  580.4 10.1 copy-start.10
  580.4 10.1 copy-start.37
  605.6 11.8 %slice-start = ((s8[16121856]{0:T(1024)(128)(4,1)}), s8[4194304]{0:T(1024)(128)(4,1)S(1)}, s32[]{:S(2)}) async-start(s8[16121856]{0:T(1024)(128)(4,1)} %bitcast.98), calls=%async_computation.6 | async-start | bytes 8388608
  605.6 11.8 %slice-start.1 = ((s8[16121856]{0:T(1024)(128)(4,1)}), s8[4194304]{0:T(1024)(128)(4,1)S(1)}, s32[]{:S(2)}) async-start(s8[16121856]{0:T(1024)(128)(4,1)} %bitcast.98), calls=%async_computation.7 | async-start | bytes 8388608
  650.0 14.9 %copy-start.4 = (bf16[4,324,512]{2,0,1:T(4,128)(2,1)S(1)}, bf16[4,324,512]{2,0,1:T(4,128)(2,1)}, u32[]{:S(2)}) copy-start(bf16[4,324,512]{2,0,1:T(4,128)(2,1)} %param.7) | copy-start | bytes 3981316
  650.0 14.9 %copy-start.25 = (f32[4,324]{1,0:T(4,128)S(1)}, f32[4,324]{1,0:T(4,128)}, u32[]{:S(2)}) copy-start(f32[4,324]{1,0:T(4,128)} %copy-done.24) | copy-start | bytes 15556
  650.0 14.9 %copy-start.29 = (f32[4,324]{1,0:T(4,128)S(1)}, f32[4,324]{1,0:T(4,128)}, u32[]{:S(2)}) copy-start(f32[4,324]{1,0:T(4,128)} %copy-done.28) | copy-start | bytes 15556
  650.0 14.9 %copy-start.31 = (f32[1,512]{1,0:T(1,128)S(1)}, f32[1,512]{1,0:T(1,128)}, u32[]{:S(2)}) copy-start(f32[1,512]{1,0:T(1,128)} %copy-done.30) | copy-start | bytes 6148
  650.0 14.9 %copy-start.35 = (f32[1,512]{1,0:T(1,128)S(1)}, f32[1,512]{1,0:T(1,128)}, u32[]{:S(2)}) copy-start(f32[1,512]{1,0:T(1,128)} %copy-done.34) | copy-start | bytes 6148
  (34 other events, 185.0 us)
Sparse Core Ops, SparseCore 0:
  14.0 128.9 all-reduce.20
  146.9 60.0 all-gather.18
  210.3 57.8 all-gather.14
  272.0 68.3 all-gather.16
  343.5 67.9 all-gather.12
  684.9 319.0 all-reduce.18
where the time goes:
time: 1030 us; the launch traced here: 1020 us
  waiting for transfers between devices  445 us (43%)
  other arithmetic  259 us (25%)
  matrix products  139 us (13%)
  blocking collectives  83.8 us (8%)
  local copies, waits for them, and re-layouts  77.7 us (8%)
  between operations  15.2 us (1%)
    unnamed x8, waiting for transfers between devices  328 us
    all_gather x2, other arithmetic, per_device(): lax.all_gather(w_in[layer], ('wide', 'narrow'), axis=0, tiled=True)  133 us
    unnamed x2, blocking collectives  83.8 us
    all_gather x2, waiting for transfers between devices, per_device(): lax.all_gather(w_out[layer], ('wide', 'narrow'), axis=0, tiled=True)  78.8 us
    all_gather x2, other arithmetic, per_device(): lax.all_gather(w_out[layer], ('wide', 'narrow'), axis=0, tiled=True)  67.6 us
    unnamed x138, local copies, waits for them, and re-layouts  40.2 us
    all_gather x2, waiting for transfers between devices, per_device(): lax.all_gather(w_in[layer], ('wide', 'narrow'), axis=0, tiled=True)  37.8 us
    reduce_sum x2, other arithmetic, backward_layer(): g_in_bias = jnp.sum(grad_pre.astype(jnp.float32), axis=(0, 1))  30.7 us
  transfers between devices with their start and end apart: 6, of which 6 were waited for; matrix products, arithmetic and copies ran while one was open for 19% of the time, Pallas kernels for 0%

commit v1 on v0

v1 whole, which is shorter than its diff:
```python
import functools
import jax
import jax.numpy as jnp
from jax import lax
from jax.experimental import pallas as pl
from jax.experimental.pallas import tpu as pltpu
from jax.sharding import PartitionSpec as P

D = 512
H = 3072
P_SIZE = 324
LAYERS = 2
G = 1536
EPS = 1e-05
CW = 512
NG = G // CW
NH = H // CW
RMAX = 336
SIZES = ((112, 100), (208, 196), (336, 324))
F32 = jnp.float32
BF16 = jnp.bfloat16
O_LN1G, O_LN1S, O_INB = 0, D, 2 * D
O_LN2G, O_LN2S, O_OUTB = 2 * D + H, 2 * D + H + G, 2 * D + H + 2 * G
VUSED = 3 * D + H + 2 * G
VROWS = VUSED // 128
VPAD = (VROWS + 15) // 16 * 16
GELU_C = 0.7978845608028654
GELU_A = 0.044715
AXES = ("wide", "narrow")
VLIM = 60 * 2**20
PART_FIELDS = {"a": (0, 1, 6), "d": (2, 3, 7), "b": (4, 5, 8, 9)}
PART_DIMS = {"a": ("y", "x", "z"), "d": ("x", "y", "z"), "b": ("z", "y", "x")}
PARTS = ("a", "d", "b")


class Layout:
    def __init__(self, mesh_shape, sp_shard, vec_shard):
        wide, narrow = mesh_shape
        self.size = {"core": 2, "x": 2, "z": wide // 4, "y": narrow}
        self.count = wide * narrow
        self.rows = D // self.count
        self.sp_shard, self.vec_shard = sp_shard, vec_shard
        self.sp_rows = (sp_shard + 2 * P_SIZE - 2) // P_SIZE
        self.vec_rows = (vec_shard + 2 * 128 - 2) // 128
        self.native = self.rows % 16 == 0
        self.small = (self.sp_rows + self.vec_rows + 7) // 8 * 8

    def part_rows(self, part):
        return sum(self.small if f == 9 else self.rows for f in PART_FIELDS[part])

    def offsets(self, part):
        spots, at = [], 0
        for f in PART_FIELDS[part]:
            spots.append((f, at))
            at += self.small if f == 9 else self.rows
        return spots

    def index(self, at):
        return ((at["z"] * 2 + at["x"]) * 2 + at["core"]) * self.size["y"] + at["y"]

    def coords(self, i):
        y, wide = i % self.size["y"], i // self.size["y"]
        return {"core": wide % 2, "x": wide // 2 % 2, "z": wide // 4, "y": y}

    def shift(self, value, axis, step=1):
        pairs = []
        for i in range(self.count):
            at = self.coords(i)
            at[axis] = (at[axis] + step) % self.size[axis]
            pairs.append((i, self.index(at)))
        return lax.ppermute(value, AXES, pairs)


def dot(a, b):
    return lax.dot_general(a, b, (((1,), (0,)), ((), ())), preferred_element_type=F32)


def dot_nt(a, b):
    return lax.dot_general(a, b, (((1,), (1,)), ((), ())), preferred_element_type=F32)


def gelu_both(z, need_grad):
    z2 = z * z
    t = jnp.tanh(z * (GELU_C + (GELU_C * GELU_A) * z2))
    w = 0.5 * t + 0.5
    h = z * w
    if not need_grad:
        return h, None
    return h, w + (h - h * w) * (2.0 * GELU_C + (6.0 * GELU_C * GELU_A) * z2)


def rows_sum8(x):
    rows, cols = x.shape
    return jnp.sum(x.reshape(rows // 8, 8, cols), axis=0)


def picker(lay, rows, cols, first, per, length, width):
    r = lax.broadcasted_iota(jnp.int32, (rows, cols), 0)
    c = lax.broadcasted_iota(jnp.int32, (rows, cols), 1)
    i, t = c // lay.small, c % lay.small - first
    hit = (t >= 0) & (t < per) & (r == (i * length) // width + t)
    return jnp.where(hit, 1.0, 0.0).astype(BF16)


def unpack_small(lay, frames_ref, vec_ref, sc_refs, st_refs):
    count = lay.count * lay.small
    ms = picker(lay, RMAX, count, 0, lay.sp_rows, lay.sp_shard, P_SIZE)
    mv = picker(lay, VPAD, count, lay.sp_rows, lay.vec_rows, lay.vec_shard, 128)
    sp = dot(ms, frames_ref[:, 0:384])
    vec = dot(mv, frames_ref[:, 0:128])
    for r in range(VROWS):
        vec_ref[:, r * 128 : (r + 1) * 128] = vec[r : r + 1, :]
    sp_t = jnp.transpose(sp)
    for (rows, n), sc, st in zip(SIZES, sc_refs, st_refs):
        i = lax.broadcasted_iota(jnp.int32, (rows, rows), 0)
        j = lax.broadcasted_iota(jnp.int32, (rows, rows), 1)
        inside = (i < n) & (j < n)
        beta = sp_t[0:rows, P_SIZE : P_SIZE + 1]
        block = jnp.where(inside, sp[0:rows, 0:rows], 0.0)
        sc[...] = jnp.where((j == n) & (i < n), beta, block).astype(BF16)
        if st is not None:
            st[...] = jnp.where(inside, sp_t[0:rows, 0:rows], 0.0).astype(BF16)


def each_block(lay, part, me):
    dims = PART_DIMS[part]
    for core in range(2):
        for p in range(lay.size[dims[0]]):
            for q in range(lay.size[dims[1]]):
                for s in range(lay.size[dims[2]]):
                    yield core, (p, q, s), dict(zip(dims, (p, q, s)), core=core)


def owner(lay, me, rel, sign):
    at = {}
    for axis, k in rel.items():
        n = lay.size[axis]
        at[axis] = lax.rem(me[axis] + (k if sign > 0 else (n - k) % n), n)
    return lay.index(at)


def assemble(lay, me, piece_refs, win_ref, wout_ref, frames_ref):
    for part in PARTS:
        mine, theirs = piece_refs[part]
        for core, place, rel in each_block(lay, part, me):
            i = owner(lay, me, rel, -1)
            src = theirs if core else mine
            for f, at in lay.offsets(part):
                if f < 6:
                    win_ref[f, pl.ds(pl.multiple_of(i * 16, 16), 16), :] = src[place + (slice(at, at + 16),)]
                elif f < 9:
                    start = pl.multiple_of(i * 48 + 16 * (f - 6), 16)
                    wout_ref[pl.ds(start, 16), :] = src[place + (slice(at, at + 16),)]
                else:
                    frames_ref[pl.ds(pl.multiple_of(i * 16, 16), 16), :] = src[place + (slice(at, at + 16),)]


def forward_part(rows, n, r_ref, vec_ref, win_ref, wout_ref, sc_ref, sv, need_grad, need_out):
    valid = lax.broadcasted_iota(jnp.int32, (rows, 1), 0) < n
    r, k, xh, a = first_norm(rows, valid, r_ref, vec_ref, sv)
    tot = jnp.zeros((rows, 1), F32)
    for j in list(range(NG, NH)) + list(range(NG)):
        z = dot(a, win_ref[j]) + vec_ref[:, O_INB + j * CW : O_INB + (j + 1) * CW]
        h, hp = gelu_both(z, need_grad)
        if j >= NG:
            if need_grad:
                sv["hv"][j - NG, 0:rows, :] = hp
            sv["v"][j - NG, 0:rows, :] = h
            tot = tot + jnp.sum(h, axis=1, keepdims=True)
        else:
            if need_grad:
                sv["sh"][j, 0:rows, :] = hp
            sv["u"][j, 0:rows, :] = h
    mu2 = tot * (1.0 / G)
    ssq = jnp.zeros((rows, 1), F32)
    for j in range(NG):
        vc = sv["v"][j, 0:rows, :] - mu2
        ssq = ssq + jnp.sum(vc * vc, axis=1, keepdims=True)
    k2 = lax.rsqrt(ssq * (1.0 / G) + EPS)
    tail = rows - 16
    trow = lax.broadcasted_iota(jnp.int32, (16, 1), 0) + tail
    for j in range(NG):
        lo = j * CW
        xh2 = (sv["v"][j, 0:rows, :] - mu2) * k2
        if need_grad:
            sv["v"][j, 0:rows, :] = xh2
        q = xh2 * vec_ref[:, O_LN2G + lo : O_LN2G + lo + CW] + vec_ref[:, O_LN2S + lo : O_LN2S + lo + CW]
        sv["q"][j, 0:rows, :] = q.astype(BF16)
        qt = q[tail:rows, :]
        qt = jnp.where(trow < n, qt, jnp.where(trow == n, 1.0, 0.0))
        sv["q"][j, tail:rows, :] = qt.astype(BF16)
    o = None
    for j in range(NG):
        s = dot(sc_ref[...], sv["q"][j, 0:rows, :])
        e = (sv["u"][j, 0:rows, :] * s).astype(BF16)
        if need_grad:
            sv["sh"][j, 0:rows, :] = sv["sh"][j, 0:rows, :] * s
            sv["e"][j, 0:rows, :] = e
        if need_out:
            part = dot(e, wout_ref[j * CW : (j + 1) * CW, :])
            o = part if o is None else o + part
    if need_out:
        o = jnp.where(valid, r + (o + vec_ref[:, O_OUTB : O_OUTB + D]), 0.0)
    return valid, (k, xh, a), k2, o


def first_norm(rows, valid, r_ref, vec_ref, sv):
    if rows > P_SIZE:
        sv["r"][0:P_SIZE, :] = r_ref[0].astype(F32)
        r = sv["r"][0:rows, :]
    else:
        r = r_ref[0, 0:rows, :].astype(F32)
    r = jnp.where(valid, r, 0.0)
    mu = jnp.mean(r, axis=1, keepdims=True)
    c = r - mu
    k = lax.rsqrt(jnp.mean(c * c, axis=1, keepdims=True) + EPS)
    xh = c * k
    a = (xh * vec_ref[:, O_LN1G : O_LN1G + D] + vec_ref[:, O_LN1S : O_LN1S + D]).astype(BF16)
    return r, k, xh, a


def backward_part(rows, n, valid, norm, k2, dn_ref, vec_ref, win_ref, wout_ref, st_ref, sv, acc):
    k, xh, a = norm
    sv["xh1"][0:rows, :] = xh
    sv["at"][0:D, 0:rows] = jnp.transpose(a)
    if rows > P_SIZE:
        sv["r"][0:P_SIZE, :] = dn_ref[0].astype(F32)
        dn = sv["r"][0:rows, :]
    else:
        dn = dn_ref[0, 0:rows, :].astype(F32)
    dn = jnp.where(valid, dn, 0.0)
    do = dn.astype(BF16)
    dot_t = jnp.transpose(do)
    gvec = acc["vec"]
    gvec[:, O_OUTB : O_OUTB + D] += rows_sum8(do.astype(F32))
    for j in range(NG):
        acc["wout"][j] += dot(dot_t, sv["e"][j, 0:rows, :])
        de = dot_nt(do, wout_ref[j * CW : (j + 1) * CW, :])
        sv["dz"][j, 0:rows, :] = (de * sv["sh"][j, 0:rows, :]).astype(BF16)
        sv["ds"][j, 0:rows, :] = (de * sv["u"][j, 0:rows, :]).astype(BF16)
    gs = None
    for j in range(NG):
        part = dot_nt(sv["ds"][j, 0:rows, :], sv["q"][j, 0:rows, :])
        gs = part if gs is None else gs + part
    acc["sp"][SIZES.index((rows, n))][...] += gs
    m1 = jnp.zeros((rows, 1), F32)
    m2 = jnp.zeros((rows, 1), F32)
    for j in range(NG):
        lo = j * CW
        dq = dot(st_ref[...], sv["ds"][j, 0:rows, :])
        sv["dq"][j, 0:rows, :] = dq
        gain = vec_ref[:, O_LN2G + lo : O_LN2G + lo + CW]
        w = dq * sv["v"][j, 0:rows, :]
        gvec[:, O_LN2G + lo : O_LN2G + lo + CW] += rows_sum8(w)
        gvec[:, O_LN2S + lo : O_LN2S + lo + CW] += rows_sum8(dq)
        m1 = m1 + jnp.sum(dq * gain, axis=1, keepdims=True)
        m2 = m2 + jnp.sum(w * gain, axis=1, keepdims=True)
    m1 = m1 * (1.0 / G)
    m2 = m2 * (1.0 / G)
    for j in range(NG):
        lo = j * CW
        gain = vec_ref[:, O_LN2G + lo : O_LN2G + lo + CW]
        dv = k2 * (sv["dq"][j, 0:rows, :] * gain - m1 - sv["v"][j, 0:rows, :] * m2)
        sv["dz"][NG + j, 0:rows, :] = (dv * sv["hv"][j, 0:rows, :]).astype(BF16)
    da = None
    for j in range(NH):
        dz = sv["dz"][j, 0:rows, :]
        acc["win"][j] += dot(sv["at"][0:D, 0:rows], dz)
        gvec[:, O_INB + j * CW : O_INB + (j + 1) * CW] += rows_sum8(dz.astype(F32))
        part = dot_nt(dz, win_ref[j])
        da = part if da is None else da + part
    xh = sv["xh1"][0:rows, :]
    gain = vec_ref[:, O_LN1G : O_LN1G + D]
    w = da * xh
    gvec[:, O_LN1G : O_LN1G + D] += rows_sum8(w)
    gvec[:, O_LN1S : O_LN1S + D] += rows_sum8(da)
    t = da * gain
    mt = jnp.mean(t, axis=1, keepdims=True)
    mx = jnp.mean(w * gain, axis=1, keepdims=True)
    return dn + k * (t - mt - xh * mx)


def put_rows(ref, value, rows):
    if rows > P_SIZE:
        ref[0] = value[0:P_SIZE, :].astype(ref.dtype)
    else:
        ref[0, 0:rows, :] = value.astype(ref.dtype)
        ref[0, rows:P_SIZE, :] = jnp.zeros((P_SIZE - rows, D), ref.dtype)


def by_class(cls, fn):
    for index, (rows, n) in enumerate(SIZES):
        pl.when(cls == index)(functools.partial(fn, index, rows, n))


def gather_grads(lay, acc, sp_scratch, wout_ref, frames_ref):
    for j in range(NG):
        wout_ref[j * CW : (j + 1) * CW, :] = jnp.transpose(acc["wout"][j]).astype(BF16)
    sp_scratch[...] = jnp.zeros(sp_scratch.shape, F32)
    for (rows, n), ref in zip(SIZES, acc["sp"]):
        jj = lax.broadcasted_iota(jnp.int32, (rows, rows), 1)
        val = ref[...]
        sp_scratch[0:rows, 0:rows] += jnp.where(jj < n, val, 0.0)
        sp_scratch[0:rows, P_SIZE : P_SIZE + 1] += val[:, n : n + 1]
    whole = sp_scratch[...]
    row = lax.broadcasted_iota(jnp.int32, (RMAX, RMAX), 0)
    col = lax.broadcasted_iota(jnp.int32, (RMAX, RMAX), 1)
    ext = jnp.where(row == P_SIZE, jnp.transpose(whole), jnp.where(row < P_SIZE, whole, 0.0))
    ext = jnp.where(col < P_SIZE, ext, 0.0).astype(BF16)
    sums = jnp.sum(acc["vec"][...], axis=0, keepdims=True)
    vec = jnp.concatenate([sums[:, r * 128 : (r + 1) * 128] for r in range(VROWS)] + [jnp.zeros((VPAD - VROWS, 128), F32)], axis=0)
    count = lay.count * lay.small
    ms = picker(lay, RMAX, count, 0, lay.sp_rows, lay.sp_shard, P_SIZE)
    mv = picker(lay, VPAD, count, lay.sp_rows, lay.vec_rows, lay.vec_shard, 128)
    tn = (((0,), (0,)), ((), ()))
    frames_ref[...] = jnp.zeros(frames_ref.shape, BF16)
    frames_ref[:, 0:RMAX] = lax.dot_general(ms, ext, tn, preferred_element_type=F32).astype(BF16)
    part = lax.dot_general(mv, vec.astype(BF16), tn, preferred_element_type=F32)
    frames_ref[:, 0:128] += part.astype(BF16)


def scatter_grads(lay, me, acc, wout_ref, frames_ref, out_refs):
    for part in PARTS:
        out = out_refs[part]
        for core, place, rel in each_block(lay, part, me):
            i = owner(lay, me, rel, 1)
            for f, at in lay.offsets(part):
                spot = (core,) + place + (slice(at, at + 16),)
                if f < 6:
                    out[spot] = acc["win"][f, pl.ds(pl.multiple_of(i * 16, 16), 16), :].astype(BF16)
                elif f < 9:
                    out[spot] = wout_ref[pl.ds(pl.multiple_of(i * 48 + 16 * (f - 6), 16), 16), :]
                else:
                    out[spot] = frames_ref[pl.ds(pl.multiple_of(i * 16, 16), 16), :]


def read_me(info_ref, images):
    return {axis: info_ref[images + k] for k, axis in enumerate(("core", "x", "z", "y"))}


class Names:
    def __init__(self, refs):
        self.refs = list(refs)

    def take(self, names):
        got = dict(zip(names, self.refs))
        self.refs = self.refs[len(names) :]
        return got


def load_weights(lay, info_ref, images, given, w):
    if lay.native:
        pieces = {p: (given[p + "0"], given[p + "1"]) for p in PARTS}
        assemble(lay, read_me(info_ref, images), pieces, w["win"], w["wout"], w["frames"])


WEIGHTS = ("win", "wout", "frames")
SAVED = ("u", "sh", "v", "hv", "q", "e")


def kernel_body(lay, images, mode, info_ref, *refs):
    names = Names(refs)
    given = names.take(weight_names(lay))
    r_ref = names.take(["r"])["r"]
    saved_in = names.take(SAVED + ("k2",)) if mode == "back" else {}
    dn_ref = names.take(["dn"])["dn"] if mode != "fore" else None
    out_ref = names.take(["out"])["out"] if mode != "back" else None
    saved_out = names.take(SAVED + ("k2",)) if mode == "fore" else {}
    gr_ref = names.take(["gr"])["gr"] if mode != "fore" else None
    grad_refs = names.take(grad_names(lay)) if mode != "fore" else {}
    w = names.take(WEIGHTS) if lay.native else given
    base = names.take(["sc0", "sc1", "sc2", "r", "vec"])
    scs = [base["sc%d" % k] for k in range(3)]
    sv = {"r": base["r"]}
    sts, acc, sp_scratch = (None,) * 3, {}, None
    if mode != "fore":
        more = names.take(["st0", "st1", "st2", "ds", "dz", "dq", "xh1", "at", "awin", "awout", "as0", "as1", "as2", "avec", "spall"])
        sts = [more["st%d" % k] for k in range(3)]
        sv.update({k: more[k] for k in ("ds", "dz", "dq", "xh1", "at")})
        acc = {"win": more["awin"], "wout": more["awout"], "sp": [more["as%d" % k] for k in range(3)], "vec": more["avec"]}
        sp_scratch = more["spall"]
    if mode == "both":
        sv.update(names.take(SAVED))
    saved = saved_in or saved_out
    sv.update({k: saved[k].at[0] for k in saved if k != "k2"})
    b = pl.program_id(0)

    @pl.when(b == 0)
    def _():
        load_weights(lay, info_ref, images, given, w)
        unpack_small(lay, w["frames"], base["vec"], scs, sts)
        sv["r"][P_SIZE:RMAX, :] = jnp.zeros((RMAX - P_SIZE, D), F32)
        if mode != "fore":
            for ref in [acc["win"], acc["wout"], acc["vec"]] + acc["sp"]:
                ref[...] = jnp.zeros(ref.shape, F32)

    def one(index, rows, n):
        if mode == "back":
            valid = lax.broadcasted_iota(jnp.int32, (rows, 1), 0) < n
            _, k, xh, a = first_norm(rows, valid, r_ref, base["vec"], sv)
            norm, k2 = (k, xh, a), saved["k2"][0, 0:rows, 0:1]
        else:
            valid, norm, k2, o = forward_part(rows, n, r_ref, base["vec"], w["win"], w["wout"], scs[index], sv, True, True)
            put_rows(out_ref, o, rows)
            if mode == "fore":
                saved["k2"][0, 0:rows, :] = jnp.broadcast_to(k2, (rows, 128))
        if mode != "fore":
            grad = backward_part(rows, n, valid, norm, k2, dn_ref, base["vec"], w["win"], w["wout"], sts[index], sv, acc)
            put_rows(gr_ref, grad, rows)

    by_class(info_ref[b], one)

    if mode != "fore":

        @pl.when(b == pl.num_programs(0) - 1)
        def _():
            if lay.native:
                gather_grads(lay, acc, sp_scratch, w["wout"], w["frames"])
                scatter_grads(lay, read_me(info_ref, images), acc, w["wout"], w["frames"], grad_refs)
            else:
                gather_grads(lay, acc, sp_scratch, grad_refs["gwout"], grad_refs["gframes"])
                grad_refs["gwin"][...] = acc["win"][...].astype(BF16)


def weight_names(lay):
    return [p + c for p in PARTS for c in "01"] if lay.native else list(WEIGHTS)


def grad_names(lay):
    return list(PARTS) if lay.native else ["gwin", "gwout", "gframes"]


def image_spec():
    return pl.BlockSpec((1, P_SIZE, D), lambda b, c: (b, 0, 0))


def saved_shapes(images):
    kinds = {"u": F32, "sh": F32, "v": F32, "hv": F32, "q": BF16, "e": BF16}
    shapes = [jax.ShapeDtypeStruct((images, NG, RMAX, CW), kinds[k]) for k in SAVED]
    return shapes + [jax.ShapeDtypeStruct((images, RMAX, 128), F32)]


def saved_specs():
    spec = pl.BlockSpec((1, NG, RMAX, CW), lambda b, c: (b, 0, 0, 0))
    return [spec] * len(SAVED) + [pl.BlockSpec((1, RMAX, 128), lambda b, c: (b, 0, 0))]


def run_kernel(lay, mode, info, weights, r, saved=None, dn=None):
    images = r.shape[0]
    image = jax.ShapeDtypeStruct((images, P_SIZE, D), F32)
    whole = pl.BlockSpec(memory_space=pltpu.VMEM)
    operands = list(weights) + [r]
    in_specs = [whole] * len(weights) + [image_spec()]
    outs, out_specs = [], []
    if mode == "back":
        operands += list(saved)
        in_specs += saved_specs()
    if mode != "fore":
        operands.append(dn)
        in_specs.append(image_spec())
    if mode != "back":
        outs.append(image)
        out_specs.append(image_spec())
    if mode == "fore":
        outs += saved_shapes(images)
        out_specs += saved_specs()
    scratch = []
    if mode != "fore":
        outs.append(image)
        out_specs.append(image_spec())
        if lay.native:
            grads = [(2,) + tuple(lay.size[a] for a in PART_DIMS[p]) + (lay.part_rows(p), CW) for p in PARTS]
        else:
            grads = [(NH, D, CW), (G, D), (lay.count * lay.small, CW)]
        outs += [jax.ShapeDtypeStruct(s, BF16) for s in grads]
        out_specs += [whole] * len(grads)
    if lay.native:
        scratch += [pltpu.VMEM((NH, D, CW), BF16), pltpu.VMEM((G, D), BF16), pltpu.VMEM((lay.count * lay.small, CW), BF16)]
    big = lambda m, dt: pltpu.VMEM((m, RMAX, CW), dt)
    scratch += [pltpu.VMEM((rows, rows), BF16) for rows, _ in SIZES] + [pltpu.VMEM((RMAX, D), F32), pltpu.VMEM((1, VUSED), F32)]
    if mode != "fore":
        scratch += [pltpu.VMEM((rows, rows), BF16) for rows, _ in SIZES]
        scratch += [big(NG, BF16), big(NH, BF16), big(NG, F32), pltpu.VMEM((RMAX, D), F32), pltpu.VMEM((D, RMAX), BF16)]
        scratch += [pltpu.VMEM((NH, D, CW), F32), pltpu.VMEM((NG, D, CW), F32)]
        scratch += [pltpu.VMEM((rows, rows), F32) for rows, _ in SIZES]
        scratch += [pltpu.VMEM((8, VUSED), F32), pltpu.VMEM((RMAX, RMAX), F32)]
    if mode == "both":
        scratch += [big(NG, F32)] * 4 + [big(NG, BF16)] * 2
    return pl.pallas_call(
        functools.partial(kernel_body, lay, images, mode),
        grid_spec=pltpu.PrefetchScalarGridSpec(
            num_scalar_prefetch=1, grid=(images,), in_specs=in_specs, out_specs=out_specs, scratch_shapes=scratch
        ),
        out_shape=outs,
        compiler_params=pltpu.CompilerParams(vmem_limit_bytes=VLIM),
        name="layer_" + mode,
    )(info, *operands)


def pack_layer(lay, w_in, w_out, spatial, vectors, me):
    index = lay.index(me)
    win = w_in.reshape(lay.rows, NH, CW)
    wout = w_out.reshape(NG, lay.rows, D)
    sp_at = lax.rem(index * lay.sp_shard, P_SIZE)
    vec_at = lax.rem(index * lay.vec_shard, 128)
    sp = lax.dynamic_update_slice(jnp.zeros((lay.sp_rows * P_SIZE,), BF16), spatial, (sp_at,)).reshape(lay.sp_rows, P_SIZE)
    vec = lax.dynamic_update_slice(jnp.zeros((lay.vec_rows * 128,), BF16), vectors, (vec_at,)).reshape(lay.vec_rows, 128)
    sp = jnp.pad(sp, ((0, 0), (0, CW - P_SIZE)))
    vec = jnp.pad(vec, ((0, lay.small - lay.sp_rows - lay.vec_rows), (0, CW - 128)))
    fields = [win[:, j] for j in range(NH)] + [wout[k] for k in range(NG)] + [jnp.concatenate([sp, vec])]
    return {p: jnp.concatenate([fields[f] for f in PART_FIELDS[p]]) for p in PARTS}


def ring_gather(lay, value, axis):
    pieces = [value]
    for _ in range(lay.size[axis] - 1):
        pieces.append(lay.shift(pieces[-1], axis))
    return jnp.stack(pieces)


def gather_layer(lay, packed, me):
    got = {}
    for p in PARTS:
        value = packed[p]
        for axis in reversed(PART_DIMS[p]):
            value = ring_gather(lay, value, axis)
        got[p] = (value, lay.shift(value, "core"))
    if lay.native:
        return [a for p in PARTS for a in got[p]]
    win, wout, frames = [None] * NH, [None] * NG, None
    for p in PARTS:
        dims = ("core",) + PART_DIMS[p]
        value = jnp.stack(got[p])
        for k, axis in enumerate(dims):
            n = lay.size[axis]
            value = jnp.take(value, lax.rem(me[axis] - jnp.arange(n) + n, n), axis=k)
        order = [dims.index(a) for a in ("z", "x", "core", "y")]
        value = value.transpose(order + [4, 5]).reshape(lay.count, lay.part_rows(p), CW)
        for f, at in lay.offsets(p):
            if f < 6:
                win[f] = value[:, at : at + lay.rows].reshape(D, CW)
            elif f < 9:
                wout[f - 6] = value[:, at : at + lay.rows]
            else:
                frames = value[:, at : at + lay.small].reshape(lay.count * lay.small, CW)
    return [jnp.stack(win), jnp.stack(wout, axis=1).reshape(G, D), frames]


def ring_scatter(lay, value, axis):
    n = lay.size[axis]
    total = value[n - 1]
    for k in range(n - 2, -1, -1):
        total = lay.shift(total.astype(BF16), axis).astype(F32) + value[k].astype(F32)
    return total


def scatter_layer(lay, grads, me):
    if not lay.native:
        gwin, gwout, gframes = grads
        gwin = gwin.reshape(NH, lay.count, lay.rows, CW)
        gwout = gwout.reshape(lay.count, NG, lay.rows, D)
        gframes = gframes.reshape(lay.count, lay.small, CW)
        fields = [gwin[j] for j in range(NH)] + [gwout[:, k] for k in range(NG)] + [gframes]
        grads = []
        for p in PARTS:
            dims = ("core",) + PART_DIMS[p]
            value = jnp.concatenate([fields[f] for f in PART_FIELDS[p]], axis=1)
            value = value.reshape(lay.size["z"], 2, 2, lay.size["y"], lay.part_rows(p), CW)
            value = value.transpose([("z", "x", "core", "y").index(a) for a in dims] + [4, 5])
            for k, axis in enumerate(dims):
                n = lay.size[axis]
                value = jnp.take(value, lax.rem(me[axis] + jnp.arange(n), n), axis=k)
            grads.append(value)
    result = {}
    for p, value in zip(PARTS, grads):
        for axis in ("core",) + PART_DIMS[p]:
            value = ring_scatter(lay, value, axis)
            if axis != PART_DIMS[p][-1]:
                value = value.astype(BF16)
        result[p] = value
    return result


def unpack_grads(lay, mine, me, sp_len, vec_len):
    fields = {f: mine[p][at : at + (lay.small if f == 9 else lay.rows)] for p in PARTS for f, at in lay.offsets(p)}
    index = lay.index(me)
    gwin = jnp.stack([fields[j] for j in range(NH)], axis=1).reshape(-1)
    gwout = jnp.concatenate([fields[6 + k] for k in range(NG)]).reshape(-1)
    sp = fields[9][0 : lay.sp_rows, 0:P_SIZE].reshape(-1)
    sp = lax.dynamic_slice(sp, (lax.rem(index * lay.sp_shard, P_SIZE),), (lay.sp_shard,))
    vec = fields[9][lay.sp_rows : lay.sp_rows + lay.vec_rows, 0:128].reshape(-1)
    vec = lax.dynamic_slice(vec, (lax.rem(index * lay.vec_shard, 128),), (lay.vec_shard,))
    return gwin, gwout, sp, vec


def per_device(mesh_shape, patches, cotangent, size_class, w_in, w_out, spatial, vectors):
    lay = Layout(mesh_shape, spatial.shape[1], vectors.shape[1])
    wide, narrow = lax.axis_index("wide"), lax.axis_index("narrow")
    me = {"core": lax.rem(wide, 2), "x": lax.rem(wide // 2, 2), "z": wide // 4, "y": narrow}
    info = jnp.concatenate([size_class, jnp.stack([me[a] for a in ("core", "x", "z", "y")]).astype(jnp.int32)])
    weights = []
    for layer in range(LAYERS):
        packed = pack_layer(lay, w_in[layer], w_out[layer], spatial[layer], vectors[layer], me)
        weights.append(gather_layer(lay, packed, me))
    hidden, *saved = run_kernel(lay, "fore", info, weights[0], patches)
    outputs, grad, *grads1 = run_kernel(lay, "both", info, weights[1], hidden, dn=cotangent)
    sums1 = scatter_layer(lay, grads1, me)
    patch_grad, *grads0 = run_kernel(lay, "back", info, weights[0], patches, saved=saved, dn=grad)
    sums0 = scatter_layer(lay, grads0, me)
    flat = [unpack_grads(lay, s, me, spatial.shape[1], vectors.shape[1]) for s in (sums0, sums1)]
    result = [jnp.stack([flat[layer][k] for layer in range(LAYERS)]) for k in range(4)]
    return (outputs, patch_grad, *result)


def solution(mesh):
    shape = (mesh.shape["wide"], mesh.shape["narrow"])
    rows = P(AXES, None, None)
    flat = P(None, AXES)
    return jax.shard_map(
        functools.partial(per_device, shape),
        mesh=mesh,
        in_specs=(rows, rows, P(AXES), flat, flat, flat, flat),
        out_specs=(rows, rows, flat, flat, flat, flat),
        check_vma=False,
    )
```

time: 1030 us -> 313 us (0.30)
  waiting for transfers between devices: 445 us -> 92.8 us
  other arithmetic: 259 us -> 9.21 us
  matrix products: 139 us -> 0 us
  Pallas kernels: 0 us -> 102 us
  blocking collectives: 83.8 us -> 0 us
  starting transfers between devices: 0.24 us -> 74.2 us
  local copies, waits for them, and re-layouts: 77.7 us -> 26.4 us
  between operations: 15.2 us -> 2.31 us
    unnamed x8 -> x0, waiting for transfers between devices: 328 us -> none
    all_gather x4 -> x0, other arithmetic: 201 us -> none  [the longest x2 133 us: per_device(): lax.all_gather(w_in[layer], ('wide', 'narrow'), axis=0, tiled=True)]
    dot_general x18 -> x0, matrix products: 139 us -> none  [the longest x2 27.6 us: forward_layer(): jnp.einsum('bpd,dh->bph', normed_low, parts['w_in'], preferred_element_ty...]
    all_gather x4 -> x0, waiting for transfers between devices: 117 us -> none  [the longest x2 78.8 us: per_device(): lax.all_gather(w_out[layer], ('wide', 'narrow'), axis=0, tiled=True)]
    pallas_call x0 -> x3, Pallas kernels: none -> 102 us  [run_kernel(): pl.pallas_call(functools.partial(kernel_body, lay, images, mode), grid_sp...]
    ppermute x0 -> x72, waiting for transfers between devices: none -> 92.8 us  [shift(): return lax.ppermute(value, AXES, pairs)]
    unnamed x2 -> x0, blocking collectives: 83.8 us -> none
    ppermute x0 -> x72, starting transfers between devices: none -> 74.2 us  [shift(): return lax.ppermute(value, AXES, pairs)]
  transfers between devices with their start and end apart: 6 -> 72, of which waited for: 6 -> 31; matrix products, arithmetic and copies ran while one was open for 19% -> 4% of each run, Pallas kernels for 0% -> 7%
where the time goes in v1:
time: 313 us; the launch traced here: 307 us
  Pallas kernels  102 us (33%)
  waiting for transfers between devices  92.8 us (30%)
  starting transfers between devices  74.2 us (24%)
  local copies, waits for them, and re-layouts  26.4 us (8%)
  other arithmetic  9.21 us (3%)
    pallas_call x3, Pallas kernels, run_kernel(): pl.pallas_call(functools.partial(kernel_body, lay, images, mode), grid_sp...  102 us
    ppermute x72, waiting for transfers between devices, shift(): return lax.ppermute(value, AXES, pairs)  92.8 us
    ppermute x72, starting transfers between devices, shift(): return lax.ppermute(value, AXES, pairs)  74.2 us
    unnamed x58, local copies, waits for them, and re-layouts  18.2 us
  transfers between devices with their start and end apart: 72, of which 31 were waited for; matrix products, arithmetic and copies ran while one was open for 4% of the time, Pallas kernels for 7%

profile of v1, /device:TPU:0, one launch (start us, length us, event | category | flops | bytes accessed | tf_op | source)
XLA Modules:
  0.0 307.3 jit_solution(4104288944150265497)
XLA Ops:
  4.5 3.1 %collective-permute-start.24 = (bf16[48,512]{1,0:T(8,128)(2,1)S(1)}, bf16[48,512]{1,0:T(8,128)(2,1)S(1)}, u32[]{:S(2)}, u32[]{:S(2)}) collective-permute-start(bf16[48,512]{1,0:T(8,128)(2,1)S(1)} %get-tuple-element.101), channel_id=1, source_target_pairs={{0,8},{1,9},{2,10},{3,11},{4,12},{5,13},{6,14},{7,15},{8,16},{9,17... | collective-permute-start | bytes 147464 | tf_op jit(solution)/shard_map/ppermute | solution.py:71
  27.2 2.5 collective-permute-done.20
  30.4 5.2 %collective-permute-done.2 = bf16[48,512]{1,0:T(8,128)(2,1)S(1)} collective-permute-done((bf16[48,512]{1,0:T(8,128)(2,1)S(1)}, bf16[48,512]{1,0:T(8,128)(2,1)S(1)}, u32[]{:S(2)}, u32[]{:S(2)}) %collective-permute-start.2) | collective-permute-done | bytes 49184 | tf_op jit(solution)/shard_map/ppermute | solution.py:71
  37.9 3.4 %collective-permute-done.21 = bf16[4,48,512]{2,1,0:T(8,128)(2,1)S(1)} collective-permute-done((bf16[4,48,512]{2,1,0:T(8,128)(2,1)S(1)}, bf16[4,48,512]{2,1,0:T(8,128)(2,1)S(1)}, u32[]{:S(2)}, u32[]{:S(2)}) %collective-permute-start.21) | collective-permute-done | bytes 196640 | tf_op jit(solution)/shard_map/ppermute | solution.py:71
  44.9 3.1 %collective-permute-done.14 = bf16[2,2,64,512]{3,2,1,0:T(8,128)(2,1)S(1)} collective-permute-done((bf16[2,2,64,512]{3,2,1,0:T(8,128)(2,1)S(1)}, bf16[2,2,64,512]{3,2,1,0:T(8,128)(2,1)S(1)}, u32[]{:S(2)}, u32[]{:S(2)}) %collective-permute-start.14) | collective-permute-done | bytes 262176 | tf_op jit(solution)/shard_map/ppermute | solution.py:71
  49.4 8.2 %collective-permute-done.27 = bf16[4,48,512]{2,1,0:T(8,128)(2,1)S(1)} collective-permute-done((bf16[4,48,512]{2,1,0:T(8,128)(2,1)S(1)}, bf16[4,48,512]{2,1,0:T(8,128)(2,1)S(1)}, u32[]{:S(2)}, u32[]{:S(2)}) %collective-permute-start.27) | collective-permute-done | bytes 196640 | tf_op jit(solution)/shard_map/ppermute | solution.py:71
  61.5 3.0 collective-permute-done.9
  64.6 2.7 collective-permute-done.33
  71.5 4.7 %collective-permute-done.34 = bf16[2,2,64,512]{3,2,1,0:T(8,128)(2,1)S(1)} collective-permute-done((bf16[2,2,64,512]{3,2,1,0:T(8,128)(2,1)S(1)}, bf16[2,2,64,512]{3,2,1,0:T(8,128)(2,1)S(1)}, u32[]{:S(2)}, u32[]{:S(2)}) %collective-permute-start.34) | collective-permute-done | bytes 262176 | tf_op jit(solution)/shard_map/ppermute | solution.py:71
  82.8 22.9 %layer_fore.1 = (f32[4,324,512]{2,1,0:T(8,128)}, f32[4,3,336,512]{3,2,1,0:T(8,128)}, f32[4,3,336,512]{3,2,1,0:T(8,128)}, f32[4,3,336,512]{3,2,1,0:T(8,128)}, f32...) custom-call(s32[8]{0:T(128)} %concatenate.27.info_ref, ...), custom_call_target="tpu_custom_call" | custom-call | tf_op jit(solution)/shard_map/layer_fore/pallas_call | solution.py:489
  106.6 47.5 %layer_both.1 = (f32[4,324,512]{2,1,0:T(8,128)}, f32[4,324,512]{2,1,0:T(8,128)}, bf16[2,2,2,4,48,512]{5,4,3,2,1,0:T(8,128)(2,1)}, bf16[2,2,2,4,48,512]{5,4,3,2,1,0:T(8,128)(2,1)}, bf16[2,4,2,2,64,512]{5,4,3,2,1,0:T(8,128)(2,1)}) custom-call(s32[8]{0:T(128)} %concatenate.27.info_ref, bf16[2,2,4,48,512]{4,3,2,1,0:T(8,128)(2,1)} %copy-done.3, ...), custom_call_target="tpu_custom_call" | custom-call | tf_op jit(solution)/shard_map/layer_both/pallas_call | solution.py:489
  154.1 5.0 %copy.35 = f32[4,324,512]{2,0,1:T(4,128)} copy(f32[4,324,512]{2,1,0:T(8,128)} %get-tuple-element.46) | data formatting | bytes 5308416
  159.0 32.1 %layer_back.1 = (f32[4,324,512]{2,1,0:T(8,128)}, bf16[2,2,2,4,48,512]{5,4,3,2,1,0:T(8,128)(2,1)}, bf16[2,2,2,4,48,512]{5,4,3,2,1,0:T(8,128)(2,1)}, bf16[2,4,2,2,64,512]{5,4,3,2,1,0:T(8,128)(2,1)}) custom-call(s32[8]{0:T(128)} %concatenate.27.info_ref, bf16[2,2,4,48,512]{4,3,2,1,0:T(8,128)(2,1)} %copy-done.1, bf16[2,2,4,48,512]{4,3,2,1,0:T(8,128)(2,1)} %copy-done.4, ...), custom_call_target="tpu_custom_call" | custom-call | tf_op jit(solution)/shard_map/layer_back/pallas_call | solution.py:489
  191.1 5.1 %copy.36 = f32[4,324,512]{2,0,1:T(4,128)} copy(f32[4,324,512]{2,1,0:T(8,128)} %get-tuple-element.47) | data formatting | bytes 5308416
  202.7 15.9 %collective-permute-start.55 = (bf16[2,4,48,512]{3,2,1,0:T(8,128)(2,1)S(1)}, bf16[2,4,48,512]{3,2,1,0:T(8,128)(2,1)S(1)}, u32[]{:S(2)}, u32[]{:S(2)}) collective-permute-start(bf16[2,4,48,512]{3,2,1,0:T(8,128)(2,1)S(1)} %slice_bitcast_fusion.9), channel_id=1, source_target_pairs={{0,1},{1,0},{2,3},{3,2},{4,5},{5,4},{6,7},{7,6},{8,9},{9,8},{10,11... | collective-permute-start | bytes 1179656 | tf_op jit(solution)/shard_map/ppermute | solution.py:71
  223.3 5.9 %collective-permute-start.49 = (bf16[2,2,64,512]{3,2,1,0:T(8,128)(2,1)S(1)}, bf16[2,2,64,512]{3,2,1,0:T(8,128)(2,1)S(1)}, u32[]{:S(2)}, u32[]{:S(2)}) collective-permute-start(bf16[2,2,64,512]{3,2,1,0:T(8,128)(2,1)S(1)} %slice_bitcast_fusion.21), channel_id=1, source_target_pairs={{0,8},{1,9},{2,10},{3,11},{4,12},{5,13},{6,14},{7,15},{8,16},{9,17... | collective-permute-start | bytes 786440 | tf_op jit(solution)/shard_map/ppermute | solution.py:71
  232.2 4.7 %collective-permute-done.37 = bf16[2,4,48,512]{3,2,1,0:T(8,128)(2,1)S(1)} collective-permute-done((bf16[2,4,48,512]{3,2,1,0:T(8,128)(2,1)S(1)}, bf16[2,4,48,512]{3,2,1,0:T(8,128)(2,1)S(1)}, u32[]{:S(2)}, u32[]{:S(2)}) %collective-permute-start.37) | collective-permute-done | bytes 393248 | tf_op jit(solution)/shard_map/ppermute | solution.py:71
  248.9 7.8 %collective-permute-done.63 = bf16[48,512]{1,0:T(8,128)(2,1)S(1)} collective-permute-done((bf16[48,512]{1,0:T(8,128)(2,1)S(1)}, bf16[48,512]{1,0:T(8,128)(2,1)S(1)}, u32[]{:S(2)}, u32[]{:S(2)}) %collective-permute-start.63) | collective-permute-done | bytes 49184 | tf_op jit(solution)/shard_map/ppermute | solution.py:71
  259.3 3.4 %collective-permute-done.39 = bf16[48,512]{1,0:T(8,128)(2,1)S(1)} collective-permute-done((bf16[48,512]{1,0:T(8,128)(2,1)S(1)}, bf16[48,512]{1,0:T(8,128)(2,1)S(1)}, u32[]{:S(2)}, u32[]{:S(2)}) %collective-permute-start.39) | collective-permute-done | bytes 49184 | tf_op jit(solution)/shard_map/ppermute | solution.py:71
  264.9 4.2 %collective-permute-done.46 = bf16[48,512]{1,0:T(8,128)(2,1)S(1)} collective-permute-done((bf16[48,512]{1,0:T(8,128)(2,1)S(1)}, bf16[48,512]{1,0:T(8,128)(2,1)S(1)}, u32[]{:S(2)}, u32[]{:S(2)}) %collective-permute-start.46) | collective-permute-done | bytes 49184 | tf_op jit(solution)/shard_map/ppermute | solution.py:71
  270.1 4.8 %collective-permute-done.59 = bf16[48,512]{1,0:T(8,128)(2,1)S(1)} collective-permute-done((bf16[48,512]{1,0:T(8,128)(2,1)S(1)}, bf16[48,512]{1,0:T(8,128)(2,1)S(1)}, u32[]{:S(2)}, u32[]{:S(2)}) %collective-permute-start.59) | collective-permute-done | bytes 49184 | tf_op jit(solution)/shard_map/ppermute | solution.py:71
  275.1 6.3 %collective-permute-done.41 = bf16[48,512]{1,0:T(8,128)(2,1)S(1)} collective-permute-done((bf16[48,512]{1,0:T(8,128)(2,1)S(1)}, bf16[48,512]{1,0:T(8,128)(2,1)S(1)}, u32[]{:S(2)}, u32[]{:S(2)}) %collective-permute-start.41) | collective-permute-done | bytes 49184 | tf_op jit(solution)/shard_map/ppermute | solution.py:71
  281.9 8.0 %collective-permute-done.69 = bf16[2,2,64,512]{3,2,1,0:T(8,128)(2,1)S(1)} collective-permute-done((bf16[2,2,64,512]{3,2,1,0:T(8,128)(2,1)S(1)}, bf16[2,2,64,512]{3,2,1,0:T(8,128)(2,1)S(1)}, u32[]{:S(2)}, u32[]{:S(2)}) %collective-permute-start.69) | collective-permute-done | bytes 262176 | tf_op jit(solution)/shard_map/ppermute | solution.py:71
  299.5 2.7 collective-permute-done.53
  (334 shorter events, 92.9 us)
Async XLA Ops:
  20.1 17.6 %collective-permute-start.31 = (bf16[2,64,512]{2,1,0:T(8,128)(2,1)S(1)}, bf16[2,64,512]{2,1,0:T(8,128)(2,1)S(1)}, u32[]{:S(2)}, u32[]{:S(2)}) collective-permute-start(bf16[2,64,512]{2,1,0:T(8,128)(2,1)S(1)} %get-tuple-element.85), channel_id=1, source_target_pairs={{0,1},{1,0},{2,3},{3,2},{4,5},{5,4},{6,7},{7,6},{8,9},{9,8},{10,11... | collective-permute-start | bytes 393224 | tf_op jit(solution)/shard_map/ppermute | solution.py:71
  25.6 15.7 %collective-permute-start.26 = (bf16[48,512]{1,0:T(8,128)(2,1)S(1)}, bf16[48,512]{1,0:T(8,128)(2,1)S(1)}, u32[]{:S(2)}, u32[]{:S(2)}) collective-permute-start(bf16[48,512]{1,0:T(8,128)(2,1)S(1)} %collective-permute-done.25), channel_id=1, source_target_pairs={{0,8},{1,9},{2,10},{3,11},{4,12},{5,13},{6,14},{7,15},{8,16},{9,17... | collective-permute-start | bytes 147464 | tf_op jit(solution)/shard_map/ppermute | solution.py:71
  26.8 21.2 %collective-permute-start.8 = (bf16[48,512]{1,0:T(8,128)(2,1)S(1)}, bf16[48,512]{1,0:T(8,128)(2,1)S(1)}, u32[]{:S(2)}, u32[]{:S(2)}) collective-permute-start(bf16[48,512]{1,0:T(8,128)(2,1)S(1)} %collective-permute-done.7), channel_id=1, source_target_pairs={{0,8},{1,9},{2,10},{3,11},{4,12},{5,13},{6,14},{7,15},{8,16},{9,17... | collective-permute-start | bytes 147464 | tf_op jit(solution)/shard_map/ppermute | solution.py:71
  41.2 17.9 %collective-permute-start.32 = (bf16[2,2,64,512]{3,2,1,0:T(8,128)(2,1)S(1)}, bf16[2,2,64,512]{3,2,1,0:T(8,128)(2,1)S(1)}, u32[]{:S(2)}, u32[]{:S(2)}) collective-permute-start(bf16[2,2,64,512]{3,2,1,0:T(8,128)(2,1)S(1)} %get-tuple-element.73), channel_id=1, source_target_pairs={{0,8},{1,9},{2,10},{3,11},{4,12},{5,13},{6,14},{7,15},{8,16},{9,17... | collective-permute-start | bytes 786440 | tf_op jit(solution)/shard_map/ppermute | solution.py:71
  41.3 18.5 %collective-permute-start.22 = (bf16[2,4,48,512]{3,2,1,0:T(8,128)(2,1)S(1)}, bf16[2,4,48,512]{3,2,1,0:T(8,128)(2,1)S(1)}, u32[]{:S(2)}, u32[]{:S(2)}) collective-permute-start(bf16[2,4,48,512]{3,2,1,0:T(8,128)(2,1)S(1)} %get-tuple-element.67), channel_id=1, source_target_pairs={{0,1},{1,0},{2,3},{3,2},{4,5},{5,4},{6,7},{7,6},{8,9},{9,8},{10,11... | collective-permute-start | bytes 1179656 | tf_op jit(solution)/shard_map/ppermute | solution.py:71
  43.3 14.3 %collective-permute-start.27 = (bf16[4,48,512]{2,1,0:T(8,128)(2,1)S(1)}, bf16[4,48,512]{2,1,0:T(8,128)(2,1)S(1)}, u32[]{:S(2)}, u32[]{:S(2)}) collective-permute-start(bf16[4,48,512]{2,1,0:T(8,128)(2,1)S(1)} %get-tuple-element.77), channel_id=1, source_target_pairs={{0,1},{1,0},{2,3},{3,2},{4,5},{5,4},{6,7},{7,6},{8,9},{9,8},{10,11... | collective-permute-start | bytes 589832 | tf_op jit(solution)/shard_map/ppermute | solution.py:71
  48.0 19.9 %collective-permute-start.4 = (bf16[2,4,48,512]{3,2,1,0:T(8,128)(2,1)S(1)}, bf16[2,4,48,512]{3,2,1,0:T(8,128)(2,1)S(1)}, u32[]{:S(2)}, u32[]{:S(2)}) collective-permute-start(bf16[2,4,48,512]{3,2,1,0:T(8,128)(2,1)S(1)} %get-tuple-element.71), channel_id=1, source_target_pairs={{0,1},{1,0},{2,3},{3,2},{4,5},{5,4},{6,7},{7,6},{8,9},{9,8},{10,11... | collective-permute-start | bytes 1179656 | tf_op jit(solution)/shard_map/ppermute | solution.py:71
  59.2 17.1 %collective-permute-start.28 = (bf16[2,4,48,512]{3,2,1,0:T(8,128)(2,1)S(1)}, bf16[2,4,48,512]{3,2,1,0:T(8,128)(2,1)S(1)}, u32[]{:S(2)}, u32[]{:S(2)}) collective-permute-start(bf16[2,4,48,512]{3,2,1,0:T(8,128)(2,1)S(1)} %get-tuple-element.65), channel_id=1, source_target_pairs={{0,4},{1,5},{2,6},{3,7},{4,0},{5,1},{6,2},{7,3},{8,12},{9,13},{10,... | collective-permute-start | bytes 1179656 | tf_op jit(solution)/shard_map/ppermute | solution.py:71
  64.6 13.5 %collective-permute-start.23 = (bf16[2,2,4,48,512]{4,3,2,1,0:T(8,128)(2,1)S(1)}, bf16[2,2,4,48,512]{4,3,2,1,0:T(8,128)(2,1)S(1)}, u32[]{:S(2)}, u32[]{:S(2)}) collective-permute-start(bf16[2,2,4,48,512]{4,3,2,1,0:T(8,128)(2,1)S(1)} %pad_maximum_fusion.4.refs_0_), channel_id=1, source_target_pairs={{0,2},{1,3},{2,0},{3,1},{4,6},{5,7},{6,4},{7,5},{8,10},{9,11},{10,... | collective-permute-start | bytes 2359304 | tf_op jit(solution)/shard_map/ppermute | solution.py:71
  70.3 35.4 %collective-permute-start.5 = (bf16[2,2,4,48,512]{4,3,2,1,0:T(8,128)(2,1)S(1)}, bf16[2,2,4,48,512]{4,3,2,1,0:T(8,128)(2,1)}, u32[]{:S(2)}, u32[]{:S(2)}) collective-permute-start(bf16[2,2,4,48,512]{4,3,2,1,0:T(8,128)(2,1)S(1)} %pad_maximum_fusion.2.refs_0_), channel_id=1, source_target_pairs={{0,2},{1,3},{2,0},{3,1},{4,6},{5,7},{6,4},{7,5},{8,10},{9,11},{10,... | collective-permute-start | bytes 2359304 | tf_op jit(solution)/shard_map/ppermute | solution.py:71
  76.2 29.5 %collective-permute-start.17 = (bf16[4,2,2,64,512]{4,3,2,1,0:T(8,128)(2,1)}, bf16[4,2,2,64,512]{4,3,2,1,0:T(8,128)(2,1)}, u32[]{:S(2)}, u32[]{:S(2)}) collective-permute-start(bf16[4,2,2,64,512]{4,3,2,1,0:T(8,128)(2,1)} %pad_maximum_fusion.refs_4_), channel_id=1, source_target_pairs={{0,2},{1,3},{2,0},{3,1},{4,6},{5,7},{6,4},{7,5},{8,10},{9,11},{10,... | collective-permute-start | bytes 3145736 | tf_op jit(solution)/shard_map/ppermute | solution.py:71
  79.1 26.6 %collective-permute-start.11 = (bf16[2,2,4,48,512]{4,3,2,1,0:T(8,128)(2,1)}, bf16[2,2,4,48,512]{4,3,2,1,0:T(8,128)(2,1)S(1)}, u32[]{:S(2)}, u32[]{:S(2)}) collective-permute-start(bf16[2,2,4,48,512]{4,3,2,1,0:T(8,128)(2,1)} %pad_maximum_fusion.3.refs_2_), channel_id=1, source_target_pairs={{0,2},{1,3},{2,0},{3,1},{4,6},{5,7},{6,4},{7,5},{8,10},{9,11},{10,... | collective-permute-start | bytes 2359304 | tf_op jit(solution)/shard_map/ppermute | solution.py:71
  199.1 19.8 %collective-permute-start.36 = (bf16[2,2,4,48,512]{4,3,2,1,0:T(8,128)(2,1)S(1)}, bf16[2,2,4,48,512]{4,3,2,1,0:T(8,128)(2,1)S(1)}, u32[]{:S(2)}, u32[]{:S(2)}) collective-permute-start(bf16[2,2,4,48,512]{4,3,2,1,0:T(8,128)(2,1)S(1)} %slice_bitcast_fusion.5), channel_id=1, source_target_pairs={{0,2},{1,3},{2,0},{3,1},{4,6},{5,7},{6,4},{7,5},{8,10},{9,11},{10,... | collective-permute-start | bytes 2359304 | tf_op jit(solution)/shard_map/ppermute | solution.py:71
  199.8 20.8 %collective-permute-start.66 = (bf16[4,2,2,64,512]{4,3,2,1,0:T(8,128)(2,1)S(1)}, bf16[4,2,2,64,512]{4,3,2,1,0:T(8,128)(2,1)S(1)}, u32[]{:S(2)}, u32[]{:S(2)}) collective-permute-start(bf16[4,2,2,64,512]{4,3,2,1,0:T(8,128)(2,1)S(1)} %slice_bitcast_fusion), channel_id=1, source_target_pairs={{0,2},{1,3},{2,0},{3,1},{4,6},{5,7},{6,4},{7,5},{8,10},{9,11},{10,... | collective-permute-start | bytes 3145736 | tf_op jit(solution)/shard_map/ppermute | solution.py:71
  200.9 20.7 %collective-permute-start.48 = (bf16[4,2,2,64,512]{4,3,2,1,0:T(8,128)(2,1)S(1)}, bf16[4,2,2,64,512]{4,3,2,1,0:T(8,128)(2,1)S(1)}, u32[]{:S(2)}, u32[]{:S(2)}) collective-permute-start(bf16[4,2,2,64,512]{4,3,2,1,0:T(8,128)(2,1)S(1)} %slice_bitcast_fusion.1), channel_id=1, source_target_pairs={{0,2},{1,3},{2,0},{3,1},{4,6},{5,7},{6,4},{7,5},{8,10},{9,11},{10,... | collective-permute-start | bytes 3145736 | tf_op jit(solution)/shard_map/ppermute | solution.py:71
  201.3 22.0 %collective-permute-start.61 = (bf16[2,4,48,512]{3,2,1,0:T(8,128)(2,1)S(1)}, bf16[2,4,48,512]{3,2,1,0:T(8,128)(2,1)S(1)}, u32[]{:S(2)}, u32[]{:S(2)}) collective-permute-start(bf16[2,4,48,512]{3,2,1,0:T(8,128)(2,1)S(1)} %slice_bitcast_fusion.7), channel_id=1, source_target_pairs={{0,4},{1,5},{2,6},{3,7},{4,0},{5,1},{6,2},{7,3},{8,12},{9,13},{10,... | collective-permute-start | bytes 1179656 | tf_op jit(solution)/shard_map/ppermute | solution.py:71
  202.7 26.6 %collective-permute-start.55 = (bf16[2,4,48,512]{3,2,1,0:T(8,128)(2,1)S(1)}, bf16[2,4,48,512]{3,2,1,0:T(8,128)(2,1)S(1)}, u32[]{:S(2)}, u32[]{:S(2)}) collective-permute-start(bf16[2,4,48,512]{3,2,1,0:T(8,128)(2,1)S(1)} %slice_bitcast_fusion.9), channel_id=1, source_target_pairs={{0,1},{1,0},{2,3},{3,2},{4,5},{5,4},{6,7},{7,6},{8,9},{9,8},{10,11... | collective-permute-start | bytes 1179656 | tf_op jit(solution)/shard_map/ppermute | solution.py:71
  220.6 16.3 %collective-permute-start.37 = (bf16[2,4,48,512]{3,2,1,0:T(8,128)(2,1)S(1)}, bf16[2,4,48,512]{3,2,1,0:T(8,128)(2,1)S(1)}, u32[]{:S(2)}, u32[]{:S(2)}) collective-permute-start(bf16[2,4,48,512]{3,2,1,0:T(8,128)(2,1)S(1)} %slice_bitcast_fusion.13), channel_id=1, source_target_pairs={{0,1},{1,0},{2,3},{3,2},{4,5},{5,4},{6,7},{7,6},{8,9},{9,8},{10,11... | collective-permute-start | bytes 1179656 | tf_op jit(solution)/shard_map/ppermute | solution.py:71
  221.6 17.5 %collective-permute-start.67 = (bf16[2,2,64,512]{3,2,1,0:T(8,128)(2,1)S(1)}, bf16[2,2,64,512]{3,2,1,0:T(8,128)(2,1)S(1)}, u32[]{:S(2)}, u32[]{:S(2)}) collective-permute-start(bf16[2,2,64,512]{3,2,1,0:T(8,128)(2,1)S(1)} %slice_bitcast_fusion.17), channel_id=1, source_target_pairs={{0,8},{1,9},{2,10},{3,11},{4,12},{5,13},{6,14},{7,15},{8,16},{9,17... | collective-permute-start | bytes 786440 | tf_op jit(solution)/shard_map/ppermute | solution.py:71
  223.3 17.3 %collective-permute-start.49 = (bf16[2,2,64,512]{3,2,1,0:T(8,128)(2,1)S(1)}, bf16[2,2,64,512]{3,2,1,0:T(8,128)(2,1)S(1)}, u32[]{:S(2)}, u32[]{:S(2)}) collective-permute-start(bf16[2,2,64,512]{3,2,1,0:T(8,128)(2,1)S(1)} %slice_bitcast_fusion.21), channel_id=1, source_target_pairs={{0,8},{1,9},{2,10},{3,11},{4,12},{5,13},{6,14},{7,15},{8,16},{9,17... | collective-permute-start | bytes 786440 | tf_op jit(solution)/shard_map/ppermute | solution.py:71
  230.7 12.6 %collective-permute-start.56 = (bf16[4,48,512]{2,1,0:T(8,128)(2,1)S(1)}, bf16[4,48,512]{2,1,0:T(8,128)(2,1)S(1)}, u32[]{:S(2)}, u32[]{:S(2)}) collective-permute-start(bf16[4,48,512]{2,1,0:T(8,128)(2,1)S(1)} %slice_bitcast_fusion.25), channel_id=1, source_target_pairs={{0,4},{1,5},{2,6},{3,7},{4,0},{5,1},{6,2},{7,3},{8,12},{9,13},{10,... | collective-permute-start | bytes 589832 | tf_op jit(solution)/shard_map/ppermute | solution.py:71
  240.6 41.0 %collective-permute-start.68 = (bf16[2,2,64,512]{3,2,1,0:T(8,128)(2,1)S(1)}, bf16[2,2,64,512]{3,2,1,0:T(8,128)(2,1)S(1)}, u32[]{:S(2)}, u32[]{:S(2)}) collective-permute-start(bf16[2,2,64,512]{3,2,1,0:T(8,128)(2,1)S(1)} %fusion.12), channel_id=1, source_target_pairs={{0,8},{1,9},{2,10},{3,11},{4,12},{5,13},{6,14},{7,15},{8,16},{9,17... | collective-permute-start | bytes 786440 | tf_op jit(solution)/shard_map/ppermute | solution.py:71
  241.1 40.6 %collective-permute-start.50 = (bf16[2,2,64,512]{3,2,1,0:T(8,128)(2,1)S(1)}, bf16[2,2,64,512]{3,2,1,0:T(8,128)(2,1)S(1)}, u32[]{:S(2)}, u32[]{:S(2)}) collective-permute-start(bf16[2,2,64,512]{3,2,1,0:T(8,128)(2,1)S(1)} %fusion.15), channel_id=1, source_target_pairs={{0,8},{1,9},{2,10},{3,11},{4,12},{5,13},{6,14},{7,15},{8,16},{9,17... | collective-permute-start | bytes 786440 | tf_op jit(solution)/shard_map/ppermute | solution.py:71
  243.3 13.4 %collective-permute-start.63 = (bf16[48,512]{1,0:T(8,128)(2,1)S(1)}, bf16[48,512]{1,0:T(8,128)(2,1)S(1)}, u32[]{:S(2)}, u32[]{:S(2)}) collective-permute-start(bf16[48,512]{1,0:T(8,128)(2,1)S(1)} %slice_bitcast_fusion.41), channel_id=1, source_target_pairs={{0,8},{1,9},{2,10},{3,11},{4,12},{5,13},{6,14},{7,15},{8,16},{9,17... | collective-permute-start | bytes 147464 | tf_op jit(solution)/shard_map/ppermute | solution.py:71
  (73 other events, 523.2 us)

commit v2 on v1

v2 whole, which is shorter than its diff:
```python
import functools
import jax
import jax.numpy as jnp
import numpy as np
from jax import lax
from jax.experimental import pallas as pl
from jax.experimental.pallas import tpu as pltpu
from jax.sharding import PartitionSpec as P

D = 512
H = 3072
P_SIZE = 324
LAYERS = 2
G = 1536
EPS = 1e-05
CW = 512
NG = G // CW
NH = H // CW
RMAX = 336
COUNTS = (100, 196, 324)
F32 = jnp.float32
BF16 = jnp.bfloat16
O_LN1G, O_LN1S, O_INB = 0, D, 2 * D
O_LN2G, O_LN2S, O_OUTB = 2 * D + H, 2 * D + H + G, 2 * D + H + 2 * G
VUSED = 3 * D + H + 2 * G
VROWS = VUSED // 128
VPAD = (VROWS + 15) // 16 * 16
GELU_C = 0.7978845608028654
GELU_A = 0.044715
AXES = ("wide", "narrow")
VLIM = 60 * 2**20
PART_FIELDS = {"a": (0, 1, 6), "d": (2, 3, 7), "b": (4, 5, 8, 9)}
PART_DIMS = {"a": ("y", "x", "z"), "d": ("x", "y", "z"), "b": ("z", "y", "x")}
PARTS = ("a", "d", "b")
PIECES = ("t00", "t01", "t10", "t11", "b00", "b01", "b10", "b11")


class Layout:
    def __init__(self, mesh_shape, sp_shard, vec_shard):
        wide, narrow = mesh_shape
        self.size = {"core": 2, "x": 2, "z": wide // 4, "y": narrow}
        self.count = wide * narrow
        self.rows = D // self.count
        self.sp_shard, self.vec_shard = sp_shard, vec_shard
        self.sp_rows = (sp_shard + 2 * P_SIZE - 2) // P_SIZE
        self.vec_rows = (vec_shard + 2 * 128 - 2) // 128
        self.native = self.rows == 16 and narrow == 2 and wide == 16
        self.small = (self.sp_rows + self.vec_rows + 7) // 8 * 8

    def part_rows(self, part):
        return sum(self.small if f == 9 else self.rows for f in PART_FIELDS[part])

    def offsets(self, part):
        spots, at = [], 0
        for f in PART_FIELDS[part]:
            spots.append((f, at))
            at += self.small if f == 9 else self.rows
        return spots

    def index(self, at):
        return ((at["z"] * 2 + at["x"]) * 2 + at["core"]) * self.size["y"] + at["y"]

    def coords(self, i):
        y, wide = i % self.size["y"], i // self.size["y"]
        return {"core": wide % 2, "x": wide // 2 % 2, "z": wide // 4, "y": y}

    def shift(self, value, axis, step=1):
        pairs = []
        for i in range(self.count):
            at = self.coords(i)
            at[axis] = (at[axis] + step) % self.size[axis]
            pairs.append((i, self.index(at)))
        return lax.ppermute(value, AXES, pairs)

    def exchange(self, value, *flips):
        pairs = []
        for i in range(self.count):
            at = self.coords(i)
            for axis, bit in flips[at["core"] % len(flips)].items():
                at[axis] ^= bit
            pairs.append((i, self.index(at)))
        return lax.ppermute(value, AXES, pairs)


CORE, NEAR, FAR = {"core": 1}, {"z": 1}, {"z": 2}
FIRST, SECOND = ({"x": 1}, {"y": 1}), ({"y": 1}, {"x": 1})


def dot(a, b):
    return lax.dot_general(a, b, (((1,), (0,)), ((), ())), preferred_element_type=F32)


def dot_nt(a, b):
    return lax.dot_general(a, b, (((1,), (1,)), ((), ())), preferred_element_type=F32)


def gelu_both(z):
    z2 = z * z
    t = jnp.tanh(z * (GELU_C + (GELU_C * GELU_A) * z2))
    w = 0.5 * t + 0.5
    h = z * w
    return h, w + (h - h * w) * (2.0 * GELU_C + (6.0 * GELU_C * GELU_A) * z2)


def rows_sum8(x):
    rows, cols = x.shape
    return jnp.sum(x.reshape(rows // 8, 8, cols), axis=0)


def picker(lay, rows, cols, first, per, length, width):
    r = lax.broadcasted_iota(jnp.int32, (rows, cols), 0)
    c = lax.broadcasted_iota(jnp.int32, (rows, cols), 1)
    i, t = c // lay.small, c % lay.small - first
    hit = (t >= 0) & (t < per) & (r == (i * length) // width + t)
    return jnp.where(hit, 1.0, 0.0).astype(BF16)


def unpack_small(lay, frames_ref, vec_ref, sc_ref, st_ref):
    count = lay.count * lay.small
    ms = picker(lay, RMAX, count, 0, lay.sp_rows, lay.sp_shard, P_SIZE)
    mv = picker(lay, VPAD, count, lay.sp_rows, lay.vec_rows, lay.vec_shard, 128)
    sp = dot(ms, frames_ref[:, 0:384])
    vec = dot(mv, frames_ref[:, 0:128])
    for r in range(VROWS):
        vec_ref[:, r * 128 : (r + 1) * 128] = vec[r : r + 1, :]
    row = lax.broadcasted_iota(jnp.int32, (RMAX, RMAX), 0)
    col = lax.broadcasted_iota(jnp.int32, (RMAX, RMAX), 1)
    inside = (row < P_SIZE) & (col < P_SIZE)
    sp = sp[:, 0:RMAX]
    sp_t = jnp.transpose(sp)
    sc_ref[...] = jnp.where(inside, sp, jnp.where((col == P_SIZE) & (row < P_SIZE), sp_t, 0.0)).astype(BF16)
    if st_ref is not None:
        st_ref[...] = jnp.where(inside, sp_t, 0.0).astype(BF16)


def role_blocks(lay, me, sign):
    for who in range(2):
        role = me["core"] ^ who
        for second in range(2):
            for first, k1, k2, core in np.ndindex(2, 2, 2, 2):
                swap = role * (first ^ second)
                at = {"z": me["z"] ^ (k1 + 2 * k2), "core": role ^ core, "x": me["x"] ^ first ^ swap, "y": me["y"] ^ second ^ swap}
                yield who, second, (first, k1, k2, core), role, lay.index(at)


def both_blocks(lay, me, sign):
    for who in range(2):
        role = me["core"] ^ who
        for k1 in range(2):
            for second, k2, first in np.ndindex(2, 2, 2):
                swap = role * (first ^ second)
                at = {"z": me["z"] ^ (k1 + 2 * k2), "core": role, "x": me["x"] ^ first ^ swap, "y": me["y"] ^ second ^ swap}
                yield who, k1, (second, k2, first), lay.index(at)


def sixteen(start):
    return pl.ds(pl.multiple_of(start, 16), 16)


def assemble(lay, me, given, win_ref, wout_ref, frames_ref):
    for who, second, place, role, i in role_blocks(lay, me, -1):
        src = given["t%d%d" % (who, second)]
        for t in range(2):
            win_ref[2 * role + t, sixteen(i * 16), :] = src[place + (slice(16 * t, 16 * t + 16),)]
        wout_ref[sixteen(i * 48 + 16 * role), :] = src[place + (slice(32, 48),)]
    for who, z, place, i in both_blocks(lay, me, -1):
        src = given["b%d%d" % (who, z)]
        for t in range(2):
            win_ref[4 + t, sixteen(i * 16), :] = src[place + (slice(16 * t, 16 * t + 16),)]
        wout_ref[sixteen(i * 48 + 32), :] = src[place + (slice(32, 48),)]
        frames_ref[sixteen(i * 16), :] = src[place + (slice(48, 64),)]


def forward_part(rows, valid, r_ref, vec_ref, win_ref, wout_ref, sc_ref, sv, save):
    h, hp = sv["h"], sv["hp"]
    r, k, xh, a = first_norm(rows, valid, r_ref, vec_ref)
    tot = jnp.zeros((rows, 1), F32)
    for j in list(range(NG, NH)) + list(range(NG)):
        z = dot(a, win_ref[j]) + vec_ref[:, O_INB + j * CW : O_INB + (j + 1) * CW]
        h[j], hpj = gelu_both(z)
        if save and j >= NG:
            sv["hv"][j - NG] = hpj.astype(BF16)
        else:
            hp[j] = hpj
        if j >= NG:
            tot = tot + jnp.sum(h[j], axis=1, keepdims=True)
    mu2 = tot * (1.0 / G)
    ssq = jnp.zeros((rows, 1), F32)
    for j in range(NG):
        vc = h[NG + j] - mu2
        ssq = ssq + jnp.sum(vc * vc, axis=1, keepdims=True)
    k2 = lax.rsqrt(ssq * (1.0 / G) + EPS)
    one = jnp.where(lax.broadcasted_iota(jnp.int32, (rows, 1), 0) == P_SIZE, 1.0, 0.0)
    for j in range(NG):
        lo = j * CW
        xh2 = (h[NG + j] - mu2) * k2
        sv["v"][j] = xh2.astype(sv["v"].dtype)
        q = xh2 * vec_ref[:, O_LN2G + lo : O_LN2G + lo + CW] + vec_ref[:, O_LN2S + lo : O_LN2S + lo + CW]
        sv["q"][j] = jnp.where(valid, q, one).astype(BF16)
    o = None
    for j in range(NG):
        s = dot(sc_ref[...], sv["q"][j])
        u = h[j]
        e = (u * s).astype(BF16)
        sv["sh"][j] = (hp[j] * s).astype(sv["sh"].dtype)
        sv["e"][j] = e
        if save:
            sv["u"][j] = u.astype(BF16)
        part = dot(e, wout_ref[j * CW : (j + 1) * CW, :])
        o = part if o is None else o + part
    o = jnp.where(valid, r + (o + vec_ref[:, O_OUTB : O_OUTB + D]), 0.0)
    return (k, xh, a), k2, o


def first_norm(rows, valid, r_ref, vec_ref):
    r = jnp.where(valid, r_ref[0, 0:rows, :].astype(F32), 0.0)
    mu = jnp.mean(r, axis=1, keepdims=True)
    c = r - mu
    k = lax.rsqrt(jnp.mean(c * c, axis=1, keepdims=True) + EPS)
    xh = c * k
    a = (xh * vec_ref[:, O_LN1G : O_LN1G + D] + vec_ref[:, O_LN1S : O_LN1S + D]).astype(BF16)
    return r, k, xh, a


def backward_part(rows, valid, norm, k2, dn_ref, vec_ref, win_ref, wout_ref, st_ref, sv, acc):
    k, xh, a = norm
    sv["xh1"][0:rows, :] = xh
    sv["at"][0:D, 0:rows] = jnp.transpose(a)
    dn = jnp.where(valid, dn_ref[0, 0:rows, :].astype(F32), 0.0)
    do = dn.astype(BF16)
    dot_t = jnp.transpose(do)
    gvec = acc["vec"]
    gvec[:, O_OUTB : O_OUTB + D] += rows_sum8(do.astype(F32))
    for j in range(NG):
        acc["wout"][j] += dot(dot_t, sv["e"][j, 0:rows, :])
        de = dot_nt(do, wout_ref[j * CW : (j + 1) * CW, :])
        sv["dz"][j, 0:rows, :] = (de * sv["sh"][j].astype(F32)).astype(BF16)
        sv["ds"][j, 0:rows, :] = (de * sv["u"][j].astype(F32)).astype(BF16)
    gs = None
    for j in range(NG):
        part = dot_nt(sv["ds"][j, 0:rows, :], sv["q"][j, 0:rows, :])
        gs = part if gs is None else gs + part
    acc["sp"][...] += gs
    m1 = jnp.zeros((rows, 1), F32)
    m2 = jnp.zeros((rows, 1), F32)
    for j in range(NG):
        lo = j * CW
        dq = jnp.where(valid, dot(st_ref[...], sv["ds"][j, 0:rows, :]), 0.0)
        sv["dq"][j, 0:rows, :] = dq
        gain = vec_ref[:, O_LN2G + lo : O_LN2G + lo + CW]
        w = dq * sv["v"][j].astype(F32)
        gvec[:, O_LN2G + lo : O_LN2G + lo + CW] += rows_sum8(w)
        gvec[:, O_LN2S + lo : O_LN2S + lo + CW] += rows_sum8(dq)
        m1 = m1 + jnp.sum(dq * gain, axis=1, keepdims=True)
        m2 = m2 + jnp.sum(w * gain, axis=1, keepdims=True)
    m1 = m1 * (1.0 / G)
    m2 = m2 * (1.0 / G)
    for j in range(NG):
        lo = j * CW
        gain = vec_ref[:, O_LN2G + lo : O_LN2G + lo + CW]
        dv = k2 * (sv["dq"][j, 0:rows, :] * gain - m1 - sv["v"][j].astype(F32) * m2)
        sv["dz"][NG + j, 0:rows, :] = (dv * sv["hv"][j].astype(F32)).astype(BF16)
    da = None
    for j in range(NH):
        dz = sv["dz"][j, 0:rows, :]
        acc["win"][j] += dot(sv["at"][0:D, 0:rows], dz)
        gvec[:, O_INB + j * CW : O_INB + (j + 1) * CW] += rows_sum8(dz.astype(F32))
        part = dot_nt(dz, win_ref[j])
        da = part if da is None else da + part
    xh = sv["xh1"][0:rows, :]
    gain = vec_ref[:, O_LN1G : O_LN1G + D]
    w = da * xh
    gvec[:, O_LN1G : O_LN1G + D] += rows_sum8(w)
    gvec[:, O_LN1S : O_LN1S + D] += rows_sum8(da)
    t = da * gain
    mt = jnp.mean(t, axis=1, keepdims=True)
    mx = jnp.mean(w * gain, axis=1, keepdims=True)
    return dn + k * (t - mt - xh * mx)


def gather_grads(lay, acc, wout_ref, frames_ref):
    for j in range(NG):
        wout_ref[j * CW : (j + 1) * CW, :] = jnp.transpose(acc["wout"][j]).astype(BF16)
    whole = acc["sp"][...]
    row = lax.broadcasted_iota(jnp.int32, (RMAX, RMAX), 0)
    col = lax.broadcasted_iota(jnp.int32, (RMAX, RMAX), 1)
    ext = jnp.where(row == P_SIZE, jnp.transpose(whole), jnp.where(row < P_SIZE, whole, 0.0))
    ext = jnp.where(col < P_SIZE, ext, 0.0).astype(BF16)
    sums = jnp.sum(acc["vec"][...], axis=0, keepdims=True)
    vec = jnp.concatenate([sums[:, r * 128 : (r + 1) * 128] for r in range(VROWS)] + [jnp.zeros((VPAD - VROWS, 128), F32)], axis=0)
    count = lay.count * lay.small
    ms = picker(lay, RMAX, count, 0, lay.sp_rows, lay.sp_shard, P_SIZE)
    mv = picker(lay, VPAD, count, lay.sp_rows, lay.vec_rows, lay.vec_shard, 128)
    tn = (((0,), (0,)), ((), ()))
    frames_ref[...] = jnp.zeros(frames_ref.shape, BF16)
    frames_ref[:, 0:RMAX] = lax.dot_general(ms, ext, tn, preferred_element_type=F32).astype(BF16)
    part = lax.dot_general(mv, vec.astype(BF16), tn, preferred_element_type=F32)
    frames_ref[:, 0:128] += part.astype(BF16)


def scatter_grads(lay, me, acc, wout_ref, frames_ref, out):
    for who, second, place, role, i in role_blocks(lay, me, 1):
        dst = out["t%d%d" % (who, second)]
        for t in range(2):
            dst[place + (slice(16 * t, 16 * t + 16),)] = acc["win"][2 * role + t, sixteen(i * 16), :].astype(BF16)
        dst[place + (slice(32, 48),)] = wout_ref[sixteen(i * 48 + 16 * role), :]
    for who, z, place, i in both_blocks(lay, me, 1):
        dst, spot = out["b%d%d" % (who, z)], place
        for t in range(2):
            dst[spot + (slice(16 * t, 16 * t + 16),)] = acc["win"][4 + t, sixteen(i * 16), :].astype(BF16)
        dst[spot + (slice(32, 48),)] = wout_ref[sixteen(i * 48 + 32), :]
        dst[spot + (slice(48, 64),)] = frames_ref[sixteen(i * 16), :]


def read_me(info_ref, images):
    return {axis: info_ref[images + k] for k, axis in enumerate(("core", "x", "z", "y"))}


class Names:
    def __init__(self, refs):
        self.refs = list(refs)

    def take(self, names):
        got = dict(zip(names, self.refs))
        self.refs = self.refs[len(names) :]
        return got


WEIGHTS = ("win", "wout", "frames")
SAVED = ("u", "sh", "v", "hv", "q", "e")


def kernel_body(lay, images, mode, scratch_names, info_ref, *refs):
    names = Names(refs)
    given = names.take(weight_names(lay))
    r_ref = names.take(["r"])["r"]
    saved = names.take(SAVED + ("k2",)) if mode == "back" else {}
    dn_ref = names.take(["dn"])["dn"] if mode != "fore" else None
    out_ref = names.take(["out"])["out"] if mode != "back" else None
    if mode == "fore":
        saved = names.take(SAVED + ("k2",))
    gr_ref = names.take(["gr"])["gr"] if mode != "fore" else None
    grad_refs = names.take(grad_names(lay)) if mode != "fore" else {}
    sv = names.take(scratch_names)
    w = sv if lay.native else given
    sv.update({k: saved[k].at[0] for k in saved})
    if mode == "both":
        sv.update(u=sv["h"], sh=sv["hp"], v=sv["h"].at[NG:NH], hv=sv["hp"].at[NG:NH])
    acc = {k: sv.get("a" + k) for k in ("win", "wout", "sp", "vec")}
    b = pl.program_id(0)

    @pl.when(b == 0)
    def _():
        if lay.native:
            assemble(lay, read_me(info_ref, images), given, w["win"], w["wout"], w["frames"])
        unpack_small(lay, w["frames"], sv["vec"], sv["sc"], sv.get("st"))
        if mode != "fore":
            for ref in acc.values():
                ref[...] = jnp.zeros(ref.shape, F32)

    cls = info_ref[b]
    n = jnp.where(cls == 0, COUNTS[0], jnp.where(cls == 1, COUNTS[1], COUNTS[2]))
    valid = lax.broadcasted_iota(jnp.int32, (RMAX, 1), 0) < n
    if mode == "back":
        _, k, xh, a = first_norm(RMAX, valid, r_ref, sv["vec"])
        norm, k2 = (k, xh, a), sv["k2"][:, 0:1]
    else:
        norm, k2, o = forward_part(RMAX, valid, r_ref, sv["vec"], w["win"], w["wout"], sv["sc"], sv, mode == "fore")
        out_ref[0] = o
        if mode == "fore":
            sv["k2"][...] = jnp.broadcast_to(k2, (RMAX, 128))
    if mode != "fore":
        gr_ref[0] = backward_part(RMAX, valid, norm, k2, dn_ref, sv["vec"], w["win"], w["wout"], sv["st"], sv, acc)

        @pl.when(b == pl.num_programs(0) - 1)
        def _():
            if lay.native:
                gather_grads(lay, acc, w["wout"], w["frames"])
                scatter_grads(lay, read_me(info_ref, images), acc, w["wout"], w["frames"], grad_refs)
            else:
                gather_grads(lay, acc, grad_refs["gwout"], grad_refs["gframes"])
                grad_refs["gwin"][...] = acc["win"][...].astype(BF16)


def scratch_for(lay, mode):
    big = lambda m, dt: pltpu.VMEM((m, RMAX, CW), dt)
    wide = lambda dt: pltpu.VMEM((RMAX, D), dt)
    made = {}
    if lay.native:
        made.update(win=pltpu.VMEM((NH, D, CW), BF16), wout=pltpu.VMEM((G, D), BF16), frames=pltpu.VMEM((lay.count * lay.small, CW), BF16))
    made.update(vec=pltpu.VMEM((1, VUSED), F32), sc=pltpu.VMEM((RMAX, RMAX), BF16))
    if mode != "back":
        made.update(h=big(NH, F32), hp=big(NH, F32))
    if mode == "both":
        made.update(q=big(NG, BF16), e=big(NG, BF16))
    if mode != "fore":
        made.update(st=pltpu.VMEM((RMAX, RMAX), BF16), ds=big(NG, BF16), dz=big(NH, BF16), dq=big(NG, F32), xh1=wide(F32))
        made.update(at=pltpu.VMEM((D, RMAX), BF16), awin=pltpu.VMEM((NH, D, CW), F32), awout=pltpu.VMEM((NG, D, CW), F32))
        made.update(asp=pltpu.VMEM((RMAX, RMAX), F32), avec=pltpu.VMEM((8, VUSED), F32))
    return made


def weight_names(lay):
    if not lay.native:
        return list(WEIGHTS)
    return list(PIECES)


def grad_names(lay):
    return list(PIECES) if lay.native else ["gwin", "gwout", "gframes"]


def image_spec():
    return pl.BlockSpec((1, RMAX, D), lambda b, c: (b, 0, 0))


def saved_shapes(images):
    shapes = [jax.ShapeDtypeStruct((images, NG, RMAX, CW), BF16) for _ in SAVED]
    return shapes + [jax.ShapeDtypeStruct((images, RMAX, 128), F32)]


def saved_specs():
    spec = pl.BlockSpec((1, NG, RMAX, CW), lambda b, c: (b, 0, 0, 0))
    return [spec] * len(SAVED) + [pl.BlockSpec((1, RMAX, 128), lambda b, c: (b, 0, 0))]


def run_kernel(lay, mode, info, weights, r, saved=None, dn=None):
    images = r.shape[0]
    image = jax.ShapeDtypeStruct((images, RMAX, D), F32)
    whole = pl.BlockSpec(memory_space=pltpu.VMEM)
    operands = list(weights) + [r]
    in_specs = [whole] * len(weights) + [image_spec()]
    outs, out_specs = [], []
    if mode == "back":
        operands += list(saved)
        in_specs += saved_specs()
    if mode != "fore":
        operands.append(dn)
        in_specs.append(image_spec())
    if mode != "back":
        outs.append(image)
        out_specs.append(image_spec())
    if mode == "fore":
        outs += saved_shapes(images)
        out_specs += saved_specs()
    if mode != "fore":
        outs.append(image)
        out_specs.append(image_spec())
        if lay.native:
            grads = [(2, 2, 2, 2, lay.part_rows("a"), CW)] * 4 + [(2, 2, 2, lay.part_rows("b"), CW)] * 4
        else:
            grads = [(NH, D, CW), (G, D), (lay.count * lay.small, CW)]
        outs += [jax.ShapeDtypeStruct(s, BF16) for s in grads]
        out_specs += [whole] * len(grads)
    scratch = scratch_for(lay, mode)
    return pl.pallas_call(
        functools.partial(kernel_body, lay, images, mode, list(scratch)),
        grid_spec=pltpu.PrefetchScalarGridSpec(
            num_scalar_prefetch=1, grid=(images,), in_specs=in_specs, out_specs=out_specs, scratch_shapes=list(scratch.values())
        ),
        out_shape=outs,
        compiler_params=pltpu.CompilerParams(vmem_limit_bytes=VLIM),
        name="layer_" + mode,
    )(info, *operands)


def pack_layer(lay, w_in, w_out, spatial, vectors, me):
    index = lay.index(me)
    win = w_in.reshape(lay.rows, NH, CW)
    wout = w_out.reshape(NG, lay.rows, D)
    sp_at = lax.rem(index * lay.sp_shard, P_SIZE)
    vec_at = lax.rem(index * lay.vec_shard, 128)
    sp = lax.dynamic_update_slice(jnp.zeros((lay.sp_rows * P_SIZE,), BF16), spatial, (sp_at,)).reshape(lay.sp_rows, P_SIZE)
    vec = lax.dynamic_update_slice(jnp.zeros((lay.vec_rows * 128,), BF16), vectors, (vec_at,)).reshape(lay.vec_rows, 128)
    sp = jnp.pad(sp, ((0, 0), (0, CW - P_SIZE)))
    vec = jnp.pad(vec, ((0, lay.small - lay.sp_rows - lay.vec_rows), (0, CW - 128)))
    fields = [win[:, j] for j in range(NH)] + [wout[k] for k in range(NG)] + [jnp.concatenate([sp, vec])]
    return {p: jnp.concatenate([fields[f] for f in PART_FIELDS[p]]) for p in PARTS}


def ring_gather(lay, value, axis):
    pieces = [value]
    for _ in range(lay.size[axis] - 1):
        pieces.append(lay.shift(pieces[-1], axis))
    return pieces


def hold(*values):
    return lax.optimization_barrier(values)


def move(lay, *items):
    values = hold(*[value for value, _ in items])
    return hold(*[lay.exchange(value, *flips) for value, (_, flips) in zip(values, items)])


def gather_start(lay, packed, me):
    even = me["core"] == 0
    keep = jnp.where(even, packed["a"], packed["d"])
    give = jnp.where(even, packed["d"], packed["a"])
    return jnp.stack([keep, lay.exchange(give, CORE)]), packed["b"]


GATHER_T = ((FAR,), (NEAR,), FIRST, SECOND)
GATHER_B = (FIRST, (FAR,), SECOND, (NEAR,))


def gather_plain(lay, packed, me):
    win, wout, frames = [None] * NH, [None] * NG, None
    for p in PARTS:
        dims = ("core",) + PART_DIMS[p]
        value = packed[p]
        for axis in reversed(dims):
            value = jnp.stack(ring_gather(lay, value, axis))
        for k, axis in enumerate(dims):
            n = lay.size[axis]
            value = jnp.take(value, lax.rem(me[axis] - jnp.arange(n) + n, n), axis=k)
        order = [dims.index(a) for a in ("z", "x", "core", "y")]
        value = value.transpose(order + [4, 5]).reshape(lay.count, lay.part_rows(p), CW)
        for f, at in lay.offsets(p):
            if f < 6:
                win[f] = value[:, at : at + lay.rows].reshape(D, CW)
            elif f < 9:
                wout[f - 6] = value[:, at : at + lay.rows]
            else:
                frames = value[:, at : at + lay.small].reshape(lay.count * lay.small, CW)
    return [jnp.stack(win), jnp.stack(wout, axis=1).reshape(G, D), frames]


def ring_scatter(lay, value, axis):
    n = lay.size[axis]
    total = value[n - 1].astype(F32)
    for k in range(n - 2, -1, -1):
        total = lay.shift(total.astype(BF16), axis).astype(F32) + value[k].astype(F32)
    return total


def low(v):
    return v.astype(BF16)


def add(mine, got):
    return mine.astype(F32) + got.astype(F32)


def scatter_core(lay, grads):
    t00, t01, t10, t11, b00, b01, b10, b11 = grads
    t11, b11 = move(lay, (t11, (CORE,)), (b11, (CORE,)))
    far, bfar = hold(low(add(t01, t11)), low(add(b01, b11)))
    t10, b10, far, bfar = hold(t10, b10, far, bfar)
    return far, bfar, (t00, lay.exchange(t10, CORE)), (b00, lay.exchange(b10, CORE))


SCATTER_T = (SECOND, FIRST, (NEAR,), (FAR,))
SCATTER_B = ((NEAR,), SECOND, (FAR,), FIRST)


def scatter_end(me, top, other, b):
    even = me["core"] == 0
    return {"a": jnp.where(even, top[0], other), "d": jnp.where(even, other, top[0]), "b": b}


def native_path(lay, me, info, packed, patches, cotangent):
    stack = lambda v, got: jnp.stack([v, got])
    (t0, b0), (t1, b1) = [gather_start(lay, p, me) for p in packed]
    x, y = move(lay, (t0, GATHER_T[0]), (b0, GATHER_B[0]))
    t0, b0 = stack(t0, x), stack(b0, y)
    for k in (1, 2):
        x, y, u, v = move(lay, (t0, GATHER_T[k]), (b0, GATHER_B[k]), (t1, GATHER_T[k - 1]), (b1, GATHER_B[k - 1]))
        t0, b0, t1, b1 = stack(t0, x), stack(b0, y), stack(t1, u), stack(b1, v)
    t0, b0, t1, b1 = hold(t0, b0, t1, b1)
    t0c, b0c = lay.exchange(t0, CORE), lay.exchange(b0, CORE)
    x, y, u, v = [lay.exchange(g, *f) for g, f in ((t0, SECOND), (b0, (NEAR,)), (t1, FIRST), (b1, SECOND))]
    x, y, u, v = hold(x, y, u, v)
    weights0 = [t0, x, t0c, lay.exchange(x, CORE), b0, y, b0c, lay.exchange(y, CORE)]
    t1, b1 = stack(t1, u), stack(b1, v)
    *weights0, t1, b1 = hold(*weights0, t1, b1)
    x, y, t1c, b1c = [lay.exchange(v, *f) for v, f in ((t1, SECOND), (b1, (NEAR,)), (t1, (CORE,)), (b1, (CORE,)))]
    hidden, *saved = run_kernel(lay, "fore", info, weights0, patches)
    x, y, t1c, b1c, hidden = hold(x, y, t1c, b1c, hidden)
    weights1 = [t1, x, t1c, lay.exchange(x, CORE), b1, y, b1c, lay.exchange(y, CORE)]
    outputs, grad, *grads1 = run_kernel(lay, "both", info, weights1, hidden, dn=cotangent)

    far1, bfar1, near1, bnear1 = scatter_core(lay, grads1)
    far1, bfar1, grad = hold(far1, bfar1, grad)
    x, y = lay.exchange(far1, *SECOND), lay.exchange(bfar1, NEAR)
    patch_grad, *grads0 = run_kernel(lay, "back", info, weights0, patches, saved=saved, dn=grad)
    x, y, patch_grad, outputs, *grads0 = hold(x, y, patch_grad, outputs, *grads0)
    top1, b1 = add(add(*near1), x), add(add(*bnear1), y)
    far0, bfar0, near0, bnear0 = scatter_core(lay, grads0)
    u, v = move(lay, (low(top1[1]), SCATTER_T[1]), (low(b1[1]), SCATTER_B[1]))
    top1, b1 = add(top1[0], u), add(b1[0], v)
    far0, bfar0, outputs, patch_grad = hold(far0, bfar0, outputs, patch_grad)
    x, y = lay.exchange(far0, *SECOND), lay.exchange(bfar0, NEAR)
    x, y, outputs, patch_grad = hold(x, y, tilt(outputs), tilt(patch_grad))
    top0, b0 = add(add(*near0), x), add(add(*bnear0), y)
    x, y, u, v = move(lay, *[(low(s[1]), f) for s, f in ((top0, SCATTER_T[1]), (b0, SCATTER_B[1]), (top1, SCATTER_T[2]), (b1, SCATTER_B[2]))])
    top0, b0, top1, b1 = add(top0[0], x), add(b0[0], y), add(top1[0], u), add(b1[0], v)
    x, y, u, v = move(lay, *[(low(s[1]), f) for s, f in ((top0, SCATTER_T[2]), (b0, SCATTER_B[2]), (top1, SCATTER_T[3]), (b1, SCATTER_B[3]))])
    top0, b0, top1, b1 = add(top0[0], x), add(b0[0], y), add(top1[0], u), add(b1[0], v)
    x, y, last1 = move(lay, (low(top0[1]), SCATTER_T[3]), (low(b0[1]), SCATTER_B[3]), (top1[1], (CORE,)))
    top0, b0 = add(top0[0], x), add(b0[0], y)
    last0 = lay.exchange(top0[1], CORE)
    outputs, patch_grad = outputs.transpose(1, 0, 2), patch_grad.transpose(1, 0, 2)
    return outputs, patch_grad, scatter_end(me, top0, last0, b0), scatter_end(me, top1, last1, b1)


def tilt(v):
    return v[:, :P_SIZE].transpose(1, 0, 2)


def plain_path(lay, me, info, packed, patches, cotangent):
    weights0, weights1 = [gather_plain(lay, p, me) for p in packed]
    hidden, *saved = run_kernel(lay, "fore", info, weights0, patches)
    outputs, grad, *grads1 = run_kernel(lay, "both", info, weights1, hidden, dn=cotangent)
    patch_grad, *grads0 = run_kernel(lay, "back", info, weights0, patches, saved=saved, dn=grad)
    outputs, patch_grad = outputs[:, :P_SIZE], patch_grad[:, :P_SIZE]
    return outputs, patch_grad, scatter_plain(lay, grads0, me), scatter_plain(lay, grads1, me)


def scatter_plain(lay, grads, me):
    gwin, gwout, gframes = grads
    gwin = gwin.reshape(NH, lay.count, lay.rows, CW)
    gwout = gwout.reshape(lay.count, NG, lay.rows, D)
    gframes = gframes.reshape(lay.count, lay.small, CW)
    fields = [gwin[j] for j in range(NH)] + [gwout[:, k] for k in range(NG)] + [gframes]
    result = {}
    for p in PARTS:
        dims = ("core",) + PART_DIMS[p]
        value = jnp.concatenate([fields[f] for f in PART_FIELDS[p]], axis=1)
        value = value.reshape(lay.size["z"], 2, 2, lay.size["y"], lay.part_rows(p), CW)
        value = value.transpose([("z", "x", "core", "y").index(a) for a in dims] + [4, 5])
        for k, axis in enumerate(dims):
            n = lay.size[axis]
            value = jnp.take(value, lax.rem(me[axis] + jnp.arange(n), n), axis=k)
        for axis in dims:
            value = ring_scatter(lay, value, axis)
        result[p] = value
    return result


def unpack_grads(lay, mine, me, sp_len, vec_len):
    fields = {f: mine[p][at : at + (lay.small if f == 9 else lay.rows)] for p in PARTS for f, at in lay.offsets(p)}
    index = lay.index(me)
    gwin = jnp.stack([fields[j] for j in range(NH)], axis=1).reshape(-1)
    gwout = jnp.concatenate([fields[6 + k] for k in range(NG)]).reshape(-1)
    sp = fields[9][0 : lay.sp_rows, 0:P_SIZE].reshape(-1)
    sp = lax.dynamic_slice(sp, (lax.rem(index * lay.sp_shard, P_SIZE),), (lay.sp_shard,))
    vec = fields[9][lay.sp_rows : lay.sp_rows + lay.vec_rows, 0:128].reshape(-1)
    vec = lax.dynamic_slice(vec, (lax.rem(index * lay.vec_shard, 128),), (lay.vec_shard,))
    return gwin, gwout, sp, vec


def per_device(mesh_shape, patches, cotangent, size_class, w_in, w_out, spatial, vectors):
    lay = Layout(mesh_shape, spatial.shape[1], vectors.shape[1])
    wide, narrow = lax.axis_index("wide"), lax.axis_index("narrow")
    me = {"core": lax.rem(wide, 2), "x": lax.rem(wide // 2, 2), "z": wide // 4, "y": narrow}
    info = jnp.concatenate([size_class, jnp.stack([me[a] for a in ("core", "x", "z", "y")]).astype(jnp.int32)])
    packed = [pack_layer(lay, w_in[l], w_out[l], spatial[l], vectors[l], me) for l in range(LAYERS)]
    spare = ((0, 0), (0, RMAX - P_SIZE), (0, 0))
    patches, cotangent = jnp.pad(patches, spare), jnp.pad(cotangent, spare)
    path = native_path if lay.native else plain_path
    outputs, patch_grad, *sums = path(lay, me, info, packed, patches, cotangent)
    flat = [unpack_grads(lay, s, me, spatial.shape[1], vectors.shape[1]) for s in sums]
    result = [jnp.stack([flat[layer][k] for layer in range(LAYERS)]) for k in range(4)]
    return (outputs, patch_grad, *result)


def solution(mesh):
    shape = (mesh.shape["wide"], mesh.shape["narrow"])
    rows = P(AXES, None, None)
    flat = P(None, AXES)
    return jax.shard_map(
        functools.partial(per_device, shape),
        mesh=mesh,
        in_specs=(rows, rows, P(AXES), flat, flat, flat, flat),
        out_specs=(rows, rows, flat, flat, flat, flat),
        check_vma=False,
    )
```

time: 313 us -> 259 us (0.83)
  starting transfers between devices: 74.2 us -> 45.6 us
  waiting for transfers between devices: 92.8 us -> 66.8 us
  Pallas kernels: 102 us -> 110 us
  local copies, waits for them, and re-layouts: 26.4 us -> 22.6 us
    ppermute x72 -> x52, starting transfers between devices: 74.2 us -> 45.6 us  [exchange(): return lax.ppermute(value, AXES, pairs)]
    ppermute x72 -> x52, waiting for transfers between devices: 92.8 us -> 66.8 us  [exchange(): return lax.ppermute(value, AXES, pairs)]
    pallas_call x3, Pallas kernels: 102 us -> 110 us  [run_kernel(): pl.pallas_call(functools.partial(kernel_body, lay, images, mode, list(scr...]
    unnamed x58 -> x76, local copies, waits for them, and re-layouts: 18.2 us -> 11.3 us
  transfers between devices with their start and end apart: 72 -> 52, of which waited for: 31 -> 16; matrix products, arithmetic and copies ran while one was open for 4% -> 6% of each run, Pallas kernels for 7% -> 24%
where the time goes in v2:
time: 259 us; the launch traced here: 256 us
  Pallas kernels  110 us (42%)
  waiting for transfers between devices  66.8 us (26%)
  starting transfers between devices  45.6 us (18%)
  local copies, waits for them, and re-layouts  22.6 us (9%)
  other arithmetic  9.05 us (3%)
    pallas_call x3, Pallas kernels, run_kernel(): pl.pallas_call(functools.partial(kernel_body, lay, images, mode, list(scr...  110 us
    ppermute x52, waiting for transfers between devices, exchange(): return lax.ppermute(value, AXES, pairs)  66.8 us
    ppermute x52, starting transfers between devices, exchange(): return lax.ppermute(value, AXES, pairs)  45.6 us
    unnamed x76, local copies, waits for them, and re-layouts  11.3 us
  transfers between devices with their start and end apart: 52, of which 16 were waited for; matrix products, arithmetic and copies ran while one was open for 6% of the time, Pallas kernels for 24%

profile of v2, /device:TPU:0, one launch (start us, length us, event | category | flops | bytes accessed | tf_op | source)
XLA Modules:
  0.0 256.0 jit_solution(7310180559656194037)
XLA Ops:
  2.1 2.1 slice_reduce_fusion
  7.9 3.0 %collective-permute-start.2 = (bf16[64,512]{1,0:T(8,128)(2,1)S(1)}, bf16[64,512]{1,0:T(8,128)(2,1)S(1)}, u32[]{:S(2)}, u32[]{:S(2)}) collective-permute-start(bf16[64,512]{1,0:T(8,128)(2,1)S(1)} %concatenate.98), channel_id=1, source_target_pairs={{0,4},{1,5},{2,3},{3,2},{4,0},{5,1},{6,7},{7,6},{8,12},{9,13},{10,... | collective-permute-start | bytes 196616 | tf_op jit(solution)/shard_map/ppermute | solution.py:82
  10.9 2.6 %collective-permute-start.1 = (bf16[2,48,512]{2,1,0:T(8,128)(2,1)S(1)}, bf16[2,48,512]{2,1,0:T(8,128)(2,1)S(1)}, u32[]{:S(2)}, u32[]{:S(2)}) collective-permute-start(bf16[2,48,512]{2,1,0:T(8,128)(2,1)S(1)} %get-tuple-element.145), channel_id=1, source_target_pairs={{0,16},{1,17},{2,18},{3,19},{4,20},{5,21},{6,22},{7,23},{8,24},{9,... | collective-permute-start | bytes 294920 | tf_op jit(solution)/shard_map/ppermute | solution.py:82
  13.6 4.9 %collective-permute-done.1 = bf16[2,48,512]{2,1,0:T(8,128)(2,1)S(1)} collective-permute-done((bf16[2,48,512]{2,1,0:T(8,128)(2,1)S(1)}, bf16[2,48,512]{2,1,0:T(8,128)(2,1)S(1)}, u32[]{:S(2)}, u32[]{:S(2)}) %collective-permute-start.1) | collective-permute-done | bytes 98336 | tf_op jit(solution)/shard_map/ppermute | solution.py:82
  19.2 3.4 %collective-permute-start.5 = (bf16[2,64,512]{2,1,0:T(8,128)(2,1)S(1)}, bf16[2,64,512]{2,1,0:T(8,128)(2,1)S(1)}, u32[]{:S(2)}, u32[]{:S(2)}) collective-permute-start(bf16[2,64,512]{2,1,0:T(8,128)(2,1)S(1)} %get-tuple-element.150), channel_id=1, source_target_pairs={{0,16},{1,17},{2,18},{3,19},{4,20},{5,21},{6,22},{7,23},{8,24},{9,... | collective-permute-start | bytes 393224 | tf_op jit(solution)/shard_map/ppermute | solution.py:82
  24.1 2.8 %collective-permute-done.7 = bf16[64,512]{1,0:T(8,128)(2,1)S(1)} collective-permute-done((bf16[64,512]{1,0:T(8,128)(2,1)S(1)}, bf16[64,512]{1,0:T(8,128)(2,1)S(1)}, u32[]{:S(2)}, u32[]{:S(2)}) %collective-permute-start.7) | collective-permute-done | bytes 65568 | tf_op jit(solution)/shard_map/ppermute | solution.py:82
  26.9 6.1 %collective-permute-done.6 = bf16[2,48,512]{2,1,0:T(8,128)(2,1)S(1)} collective-permute-done((bf16[2,48,512]{2,1,0:T(8,128)(2,1)S(1)}, bf16[2,48,512]{2,1,0:T(8,128)(2,1)S(1)}, u32[]{:S(2)}, u32[]{:S(2)}) %collective-permute-start.6) | collective-permute-done | bytes 98336 | tf_op jit(solution)/shard_map/ppermute | solution.py:82
  35.2 3.0 %collective-permute-start.11 = (bf16[2,64,512]{2,1,0:T(8,128)(2,1)S(1)}, bf16[2,64,512]{2,1,0:T(8,128)(2,1)S(1)}, u32[]{:S(2)}, u32[]{:S(2)}) collective-permute-start(bf16[2,64,512]{2,1,0:T(8,128)(2,1)S(1)} %get-tuple-element.160), channel_id=1, source_target_pairs={{0,16},{1,17},{2,18},{3,19},{4,20},{5,21},{6,22},{7,23},{8,24},{9,... | collective-permute-start | bytes 393224 | tf_op jit(solution)/shard_map/ppermute | solution.py:82
  38.2 4.3 %collective-permute-done.11 = bf16[2,64,512]{2,1,0:T(8,128)(2,1)S(1)} collective-permute-done((bf16[2,64,512]{2,1,0:T(8,128)(2,1)S(1)}, bf16[2,64,512]{2,1,0:T(8,128)(2,1)S(1)}, u32[]{:S(2)}, u32[]{:S(2)}) %collective-permute-start.11) | collective-permute-done | bytes 131104 | tf_op jit(solution)/shard_map/ppermute | solution.py:82
  47.5 13.7 %collective-permute-done.15 = bf16[2,2,64,512]{3,2,1,0:T(8,128)(2,1)S(1)} collective-permute-done((bf16[2,2,64,512]{3,2,1,0:T(8,128)(2,1)S(1)}, bf16[2,2,64,512]{3,2,1,0:T(8,128)(2,1)S(1)}, u32[]{:S(2)}, u32[]{:S(2)}) %collective-permute-start.15) | collective-permute-done | bytes 262176 | tf_op jit(solution)/shard_map/ppermute | solution.py:82
  66.9 1.8 collective-permute-start.21
  70.9 24.4 %layer_fore.1 = (f32[4,336,512]{2,1,0:T(8,128)}, bf16[4,3,336,512]{3,2,1,0:T(8,128)(2,1)}, bf16[4,3,336,512]{3,2,1,0:T(8,128)(2,1)}, bf16[4,3,336,512]{3,2,1,0:T...) custom-call(s32[8]{0:T(128)} %concatenate.87.info_ref, ...), custom_call_target="tpu_custom_call" | custom-call | tf_op jit(solution)/shard_map/layer_fore/pallas_call | solution.py:456
  101.0 48.6 %layer_both.1 = (f32[4,336,512]{2,1,0:T(8,128)}, f32[4,336,512]{2,1,0:T(8,128)}, bf16[2,2,2,2,48,512]{5,4,3,2,1,0:T(8,128)(2,1)}, bf16[2,2,2,2,48,512]{5,4,3,2,1...) custom-call(s32[8]{0:T(128)} %concatenate.87.info_ref, ...), custom_call_target="tpu_custom_call" | custom-call | tf_op jit(solution)/shard_map/layer_both/pallas_call | solution.py:456
  150.2 2.7 %collective-permute-done.27 = bf16[2,2,2,64,512]{4,3,2,1,0:T(8,128)(2,1)S(1)} collective-permute-done((bf16[2,2,2,64,512]{4,3,2,1,0:T(8,128)(2,1)}, bf16[2,2,2,64,512]{4,3,2,1,0:T(8,128)(2,1)S(1)}, u32[]{:S(2)}, u32[]{:S(2)}) %collective-permute-start.27) | collective-permute-done | bytes 524320 | tf_op jit(solution)/shard_map/ppermute | solution.py:82
  157.7 36.8 %layer_back.1 = (f32[4,336,512]{2,1,0:T(8,128)}, bf16[2,2,2,2,48,512]{5,4,3,2,1,0:T(8,128)(2,1)}, bf16[2,2,2,2,48,512]{5,4,3,2,1,0:T(8,128)(2,1)}, bf16[2,2,2,2,...) custom-call(s32[8]{0:T(128)} %concatenate.87.info_ref, ...), custom_call_target="tpu_custom_call" | custom-call | tf_op jit(solution)/shard_map/layer_back/pallas_call | solution.py:456
  198.6 7.2 %collective-permute-done.39 = bf16[2,2,64,512]{3,2,1,0:T(8,128)(2,1)S(1)} collective-permute-done((bf16[2,2,64,512]{3,2,1,0:T(8,128)(2,1)S(1)}, bf16[2,2,64,512]{3,2,1,0:T(8,128)(2,1)S(1)}, u32[]{:S(2)}, u32[]{:S(2)}) %collective-permute-start.39) | collective-permute-done | bytes 262176 | tf_op jit(solution)/shard_map/ppermute | solution.py:82
  208.5 1.8 collective-permute-start.33
  211.4 9.7 %collective-permute-done.33 = bf16[2,2,2,64,512]{4,3,2,1,0:T(8,128)(2,1)S(1)} collective-permute-done((bf16[2,2,2,64,512]{4,3,2,1,0:T(8,128)(2,1)S(1)}, bf16[2,2,2,64,512]{4,3,2,1,0:T(8,128)(2,1)S(1)}, u32[]{:S(2)}, u32[]{:S(2)}) %collective-permute-start.33) | collective-permute-done | bytes 524320 | tf_op jit(solution)/shard_map/ppermute | solution.py:82
  226.9 6.2 %collective-permute-done.43 = bf16[2,64,512]{2,1,0:T(8,128)(2,1)S(1)} collective-permute-done((bf16[2,64,512]{2,1,0:T(8,128)(2,1)S(1)}, bf16[2,64,512]{2,1,0:T(8,128)(2,1)S(1)}, u32[]{:S(2)}, u32[]{:S(2)}) %collective-permute-start.43) | collective-permute-done | bytes 131104 | tf_op jit(solution)/shard_map/ppermute | solution.py:82
  234.6 2.1 collective-permute-start.46
  238.0 3.2 %copy.33 = f32[4,324,512]{2,0,1:T(4,128)} copy(f32[4,324,512]{2,1,0:T(8,128)S(1)} %bitcast.236) | data formatting | bytes 5308416
  241.2 3.2 %copy.34 = f32[4,324,512]{2,0,1:T(4,128)} copy(f32[4,324,512]{2,1,0:T(8,128)S(1)} %bitcast.237) | data formatting | bytes 5308416
  246.5 2.4 collective-permute-done.49
  249.0 1.9 collective-permute-done.48
  (288 shorter events, 55.9 us)
Async XLA Ops:
  18.5 14.5 %collective-permute-start.4 = (bf16[2,2,48,512]{3,2,1,0:T(8,128)(2,1)S(1)}, bf16[2,2,48,512]{3,2,1,0:T(8,128)(2,1)S(1)}, u32[]{:S(2)}, u32[]{:S(2)}) collective-permute-start(bf16[2,2,48,512]{3,2,1,0:T(8,128)(2,1)S(1)} %get-tuple-element.149), channel_id=1, source_target_pairs={{0,8},{1,9},{2,10},{3,11},{4,12},{5,13},{6,14},{7,15},{8,0},{9,1},... | collective-permute-start | bytes 589832 | tf_op jit(solution)/shard_map/ppermute | solution.py:82
  19.2 13.8 %collective-permute-start.5 = (bf16[2,64,512]{2,1,0:T(8,128)(2,1)S(1)}, bf16[2,64,512]{2,1,0:T(8,128)(2,1)S(1)}, u32[]{:S(2)}, u32[]{:S(2)}) collective-permute-start(bf16[2,64,512]{2,1,0:T(8,128)(2,1)S(1)} %get-tuple-element.150), channel_id=1, source_target_pairs={{0,16},{1,17},{2,18},{3,19},{4,20},{5,21},{6,22},{7,23},{8,24},{9,... | collective-permute-start | bytes 393224 | tf_op jit(solution)/shard_map/ppermute | solution.py:82
  22.6 10.4 %collective-permute-start.6 = (bf16[2,48,512]{2,1,0:T(8,128)(2,1)S(1)}, bf16[2,48,512]{2,1,0:T(8,128)(2,1)S(1)}, u32[]{:S(2)}, u32[]{:S(2)}) collective-permute-start(bf16[2,48,512]{2,1,0:T(8,128)(2,1)S(1)} %get-tuple-element.151), channel_id=1, source_target_pairs={{0,16},{1,17},{2,18},{3,19},{4,20},{5,21},{6,22},{7,23},{8,24},{9,... | collective-permute-start | bytes 294920 | tf_op jit(solution)/shard_map/ppermute | solution.py:82
  33.2 10.4 %collective-permute-start.8 = (bf16[2,2,2,48,512]{4,3,2,1,0:T(8,128)(2,1)S(1)}, bf16[2,2,2,48,512]{4,3,2,1,0:T(8,128)(2,1)S(1)}, u32[]{:S(2)}, u32[]{:S(2)}) collective-permute-start(bf16[2,2,2,48,512]{4,3,2,1,0:T(8,128)(2,1)S(1)} %get-tuple-element.157), channel_id=1, source_target_pairs={{0,4},{1,5},{2,3},{3,2},{4,0},{5,1},{6,7},{7,6},{8,12},{9,13},{10,... | collective-permute-start | bytes 1179656 | tf_op jit(solution)/shard_map/ppermute | solution.py:82
  43.8 17.4 %collective-permute-start.12 = (bf16[2,2,2,2,48,512]{5,4,3,2,1,0:T(8,128)(2,1)S(1)}, bf16[2,2,2,2,48,512]{5,4,3,2,1,0:T(8,128)(2,1)S(1)}, u32[]{:S(2)}, u32[]{:S(2)}) collective-permute-start(bf16[2,2,2,2,48,512]{5,4,3,2,1,0:T(8,128)(2,1)S(1)} %pad_maximum_fusion.refs_0_), channel_id=1, source_target_pairs={{0,1},{1,0},{2,6},{3,7},{4,5},{5,4},{6,2},{7,3},{8,9},{9,8},{10,14... | collective-permute-start | bytes 2359304 | tf_op jit(solution)/shard_map/ppermute | solution.py:82
  45.6 15.7 %collective-permute-start.13 = (bf16[2,2,2,64,512]{4,3,2,1,0:T(8,128)(2,1)S(1)}, bf16[2,2,2,64,512]{4,3,2,1,0:T(8,128)(2,1)S(1)}, u32[]{:S(2)}, u32[]{:S(2)}) collective-permute-start(bf16[2,2,2,64,512]{4,3,2,1,0:T(8,128)(2,1)S(1)} %pad_maximum_fusion.2.refs_4_), channel_id=1, source_target_pairs={{0,8},{1,9},{2,10},{3,11},{4,12},{5,13},{6,14},{7,15},{8,0},{9,1},... | collective-permute-start | bytes 1572872 | tf_op jit(solution)/shard_map/ppermute | solution.py:82
  46.8 14.5 %collective-permute-start.14 = (bf16[2,2,2,48,512]{4,3,2,1,0:T(8,128)(2,1)S(1)}, bf16[2,2,2,48,512]{4,3,2,1,0:T(8,128)(2,1)S(1)}, u32[]{:S(2)}, u32[]{:S(2)}) collective-permute-start(bf16[2,2,2,48,512]{4,3,2,1,0:T(8,128)(2,1)S(1)} %pad_maximum_fusion.5), channel_id=1, source_target_pairs={{0,4},{1,5},{2,3},{3,2},{4,0},{5,1},{6,7},{7,6},{8,12},{9,13},{10,... | collective-permute-start | bytes 1179656 | tf_op jit(solution)/shard_map/ppermute | solution.py:82
  47.1 14.2 %collective-permute-start.15 = (bf16[2,2,64,512]{3,2,1,0:T(8,128)(2,1)S(1)}, bf16[2,2,64,512]{3,2,1,0:T(8,128)(2,1)S(1)}, u32[]{:S(2)}, u32[]{:S(2)}) collective-permute-start(bf16[2,2,64,512]{3,2,1,0:T(8,128)(2,1)S(1)} %pad_maximum_fusion.8), channel_id=1, source_target_pairs={{0,1},{1,0},{2,6},{3,7},{4,5},{5,4},{6,2},{7,3},{8,9},{9,8},{10,14... | collective-permute-start | bytes 786440 | tf_op jit(solution)/shard_map/ppermute | solution.py:82
  47.5 16.9 %collective-permute-start.16 = (bf16[2,2,2,2,48,512]{5,4,3,2,1,0:T(8,128)(2,1)S(1)}, bf16[2,2,2,2,48,512]{5,4,3,2,1,0:T(8,128)(2,1)S(1)}, u32[]{:S(2)}, u32[]{:S(2)}) collective-permute-start(bf16[2,2,2,2,48,512]{5,4,3,2,1,0:T(8,128)(2,1)S(1)} %pad_maximum_fusion.refs_0_), channel_id=1, source_target_pairs={{0,2},{1,3},{2,0},{3,1},{4,6},{5,7},{6,4},{7,5},{8,10},{9,11},{10,... | collective-permute-start | bytes 2359304 | tf_op jit(solution)/shard_map/ppermute | solution.py:82
  65.1 30.1 %collective-permute-start.22 = (bf16[2,2,2,2,48,512]{5,4,3,2,1,0:T(8,128)(2,1)S(1)}, bf16[2,2,2,2,48,512]{5,4,3,2,1,0:T(8,128)(2,1)}, u32[]{:S(2)}, u32[]{:S(2)}) collective-permute-start(bf16[2,2,2,2,48,512]{5,4,3,2,1,0:T(8,128)(2,1)S(1)} %pad_maximum_fusion.1.refs_0_), channel_id=1, source_target_pairs={{0,2},{1,3},{2,0},{3,1},{4,6},{5,7},{6,4},{7,5},{8,10},{9,11},{10,... | collective-permute-start | bytes 2359304 | tf_op jit(solution)/shard_map/ppermute | solution.py:82
  65.3 30.0 %collective-permute-start.20 = (bf16[2,2,2,2,48,512]{5,4,3,2,1,0:T(8,128)(2,1)S(1)}, bf16[2,2,2,2,48,512]{5,4,3,2,1,0:T(8,128)(2,1)}, u32[]{:S(2)}, u32[]{:S(2)}) collective-permute-start(bf16[2,2,2,2,48,512]{5,4,3,2,1,0:T(8,128)(2,1)S(1)} %pad_maximum_fusion.1.refs_0_), channel_id=1, source_target_pairs={{0,1},{1,0},{2,6},{3,7},{4,5},{5,4},{6,2},{7,3},{8,9},{9,8},{10,14... | collective-permute-start | bytes 2359304 | tf_op jit(solution)/shard_map/ppermute | solution.py:82
  66.8 28.4 %collective-permute-start.23 = (bf16[2,2,2,64,512]{4,3,2,1,0:T(8,128)(2,1)}, bf16[2,2,2,64,512]{4,3,2,1,0:T(8,128)(2,1)S(1)}, u32[]{:S(2)}, u32[]{:S(2)}) collective-permute-start(bf16[2,2,2,64,512]{4,3,2,1,0:T(8,128)(2,1)} %pad_maximum_fusion.3.refs_4_), channel_id=1, source_target_pairs={{0,2},{1,3},{2,0},{3,1},{4,6},{5,7},{6,4},{7,5},{8,10},{9,11},{10,... | collective-permute-start | bytes 1572872 | tf_op jit(solution)/shard_map/ppermute | solution.py:82
  66.9 28.4 %collective-permute-start.21 = (bf16[2,2,2,64,512]{4,3,2,1,0:T(8,128)(2,1)}, bf16[2,2,2,64,512]{4,3,2,1,0:T(8,128)(2,1)}, u32[]{:S(2)}, u32[]{:S(2)}) collective-permute-start(bf16[2,2,2,64,512]{4,3,2,1,0:T(8,128)(2,1)} %pad_maximum_fusion.3.refs_4_), channel_id=1, source_target_pairs={{0,8},{1,9},{2,10},{3,11},{4,12},{5,13},{6,14},{7,15},{8,0},{9,1},... | collective-permute-start | bytes 1572872 | tf_op jit(solution)/shard_map/ppermute | solution.py:82
  155.3 39.2 %collective-permute-start.28 = (bf16[2,2,2,2,48,512]{5,4,3,2,1,0:T(8,128)(2,1)S(1)}, bf16[2,2,2,2,48,512]{5,4,3,2,1,0:T(8,128)(2,1)S(1)}, u32[]{:S(2)}, u32[]{:S(2)}) collective-permute-start(bf16[2,2,2,2,48,512]{5,4,3,2,1,0:T(8,128)(2,1)S(1)} %add_convert_fusion.1), channel_id=1, source_target_pairs={{0,1},{1,0},{2,6},{3,7},{4,5},{5,4},{6,2},{7,3},{8,9},{9,8},{10,14... | collective-permute-start | bytes 2359304 | tf_op jit(solution)/shard_map/ppermute | solution.py:82
  156.9 37.6 %collective-permute-start.29 = (bf16[2,2,2,64,512]{4,3,2,1,0:T(8,128)(2,1)}, bf16[2,2,2,64,512]{4,3,2,1,0:T(8,128)(2,1)S(1)}, u32[]{:S(2)}, u32[]{:S(2)}) collective-permute-start(bf16[2,2,2,64,512]{4,3,2,1,0:T(8,128)(2,1)} %add_convert_fusion.3), channel_id=1, source_target_pairs={{0,8},{1,9},{2,10},{3,11},{4,12},{5,13},{6,14},{7,15},{8,0},{9,1},... | collective-permute-start | bytes 1572872 | tf_op jit(solution)/shard_map/ppermute | solution.py:82
  157.2 37.3 %collective-permute-start.37 = (bf16[2,2,2,64,512]{4,3,2,1,0:T(8,128)(2,1)}, bf16[2,2,2,64,512]{4,3,2,1,0:T(8,128)(2,1)S(1)}, u32[]{:S(2)}, u32[]{:S(2)}) collective-permute-start(bf16[2,2,2,64,512]{4,3,2,1,0:T(8,128)(2,1)} %get-tuple-element.256), channel_id=1, source_target_pairs={{0,2},{1,3},{2,0},{3,1},{4,6},{5,7},{6,4},{7,5},{8,10},{9,11},{10,... | collective-permute-start | bytes 1572872 | tf_op jit(solution)/shard_map/ppermute | solution.py:82
  157.2 37.6 %collective-permute-start.36 = (bf16[2,2,2,2,48,512]{5,4,3,2,1,0:T(8,128)(2,1)}, bf16[2,2,2,2,48,512]{5,4,3,2,1,0:T(8,128)(2,1)S(1)}, u32[]{:S(2)}, u32[]{:S(2)}) collective-permute-start(bf16[2,2,2,2,48,512]{5,4,3,2,1,0:T(8,128)(2,1)} %get-tuple-element.253), channel_id=1, source_target_pairs={{0,2},{1,3},{2,0},{3,1},{4,6},{5,7},{6,4},{7,5},{8,10},{9,11},{10,... | collective-permute-start | bytes 2359304 | tf_op jit(solution)/shard_map/ppermute | solution.py:82
  207.2 13.9 %collective-permute-start.32 = (bf16[2,2,2,2,48,512]{5,4,3,2,1,0:T(8,128)(2,1)S(1)}, bf16[2,2,2,2,48,512]{5,4,3,2,1,0:T(8,128)(2,1)S(1)}, u32[]{:S(2)}, u32[]{:S(2)}) collective-permute-start(bf16[2,2,2,2,48,512]{5,4,3,2,1,0:T(8,128)(2,1)S(1)} %add_convert_fusion), channel_id=1, source_target_pairs={{0,1},{1,0},{2,6},{3,7},{4,5},{5,4},{6,2},{7,3},{8,9},{9,8},{10,14... | collective-permute-start | bytes 2359304 | tf_op jit(solution)/shard_map/ppermute | solution.py:82
  208.5 12.6 %collective-permute-start.33 = (bf16[2,2,2,64,512]{4,3,2,1,0:T(8,128)(2,1)S(1)}, bf16[2,2,2,64,512]{4,3,2,1,0:T(8,128)(2,1)S(1)}, u32[]{:S(2)}, u32[]{:S(2)}) collective-permute-start(bf16[2,2,2,64,512]{4,3,2,1,0:T(8,128)(2,1)S(1)} %add_convert_fusion.2), channel_id=1, source_target_pairs={{0,8},{1,9},{2,10},{3,11},{4,12},{5,13},{6,14},{7,15},{8,0},{9,1},... | collective-permute-start | bytes 1572872 | tf_op jit(solution)/shard_map/ppermute | solution.py:82
  210.4 10.8 %collective-permute-start.35 = (bf16[2,2,2,64,512]{4,3,2,1,0:T(8,128)(2,1)S(1)}, bf16[2,2,2,64,512]{4,3,2,1,0:T(8,128)(2,1)S(1)}, u32[]{:S(2)}, u32[]{:S(2)}) collective-permute-start(bf16[2,2,2,64,512]{4,3,2,1,0:T(8,128)(2,1)S(1)} %copy-done.28), channel_id=1, source_target_pairs={{0,2},{1,3},{2,0},{3,1},{4,6},{5,7},{6,4},{7,5},{8,10},{9,11},{10,... | collective-permute-start | bytes 1572872 | tf_op jit(solution)/shard_map/ppermute | solution.py:82
  210.4 11.0 %collective-permute-start.34 = (bf16[2,2,2,2,48,512]{5,4,3,2,1,0:T(8,128)(2,1)S(1)}, bf16[2,2,2,2,48,512]{5,4,3,2,1,0:T(8,128)(2,1)S(1)}, u32[]{:S(2)}, u32[]{:S(2)}) collective-permute-start(bf16[2,2,2,2,48,512]{5,4,3,2,1,0:T(8,128)(2,1)S(1)} %copy-done.26), channel_id=1, source_target_pairs={{0,2},{1,3},{2,0},{3,1},{4,6},{5,7},{6,4},{7,5},{8,10},{9,11},{10,... | collective-permute-start | bytes 2359304 | tf_op jit(solution)/shard_map/ppermute | solution.py:82
  221.8 11.3 %collective-permute-start.40 = (bf16[2,2,2,48,512]{4,3,2,1,0:T(8,128)(2,1)S(1)}, bf16[2,2,2,48,512]{4,3,2,1,0:T(8,128)(2,1)S(1)}, u32[]{:S(2)}, u32[]{:S(2)}) collective-permute-start(bf16[2,2,2,48,512]{4,3,2,1,0:T(8,128)(2,1)S(1)} %fusion.4), channel_id=1, source_target_pairs={{0,4},{1,5},{2,3},{3,2},{4,0},{5,1},{6,7},{7,6},{8,12},{9,13},{10,... | collective-permute-start | bytes 1179656 | tf_op jit(solution)/shard_map/ppermute | solution.py:82
  233.5 10.9 %collective-permute-start.44 = (bf16[2,2,48,512]{3,2,1,0:T(8,128)(2,1)S(1)}, bf16[2,2,48,512]{3,2,1,0:T(8,128)(2,1)S(1)}, u32[]{:S(2)}, u32[]{:S(2)}) collective-permute-start(bf16[2,2,48,512]{3,2,1,0:T(8,128)(2,1)S(1)} %fusion.13), channel_id=1, source_target_pairs={{0,8},{1,9},{2,10},{3,11},{4,12},{5,13},{6,14},{7,15},{8,0},{9,1},... | collective-permute-start | bytes 589832 | tf_op jit(solution)/shard_map/ppermute | solution.py:82
  233.7 10.7 %collective-permute-start.45 = (bf16[2,64,512]{2,1,0:T(8,128)(2,1)S(1)}, bf16[2,64,512]{2,1,0:T(8,128)(2,1)S(1)}, u32[]{:S(2)}, u32[]{:S(2)}) collective-permute-start(bf16[2,64,512]{2,1,0:T(8,128)(2,1)S(1)} %fusion.17), channel_id=1, source_target_pairs={{0,16},{1,17},{2,18},{3,19},{4,20},{5,21},{6,22},{7,23},{8,24},{9,... | collective-permute-start | bytes 393224 | tf_op jit(solution)/shard_map/ppermute | solution.py:82
  (58 other events, 395.9 us)
